TPU v7x, 256 devices: a whole 4x4x8 slice. The times are simulated.
256 devices in a mesh: lat: 64 (over z, x_lo, y), lon: 4 (over x_hi, core).
Axes of the slice: x: 4 (x_hi: 2, x_lo: 2; x = x_hi * 2 + x_lo), y: 4, z: 8, core: 2. Of those that a mesh axis runs over, the one named last changes fastest.
Arguments:
- tokens: bfloat16 [768, 96, 2, 512], P('lat', 'lon'), may hold values from -6 to 6
- land_sea: int32 [768, 96], P('lat', 'lon'), may hold values from 0 to 2
- surface_embed: float32 [3, 512], replicated, may hold values from -4 to 4
- level_table: int32 [2], replicated, may hold values from 0 to 12
- level_embed: float32 [13, 512], replicated, may hold values from -4 to 4
- gain1: float32 [512], replicated, may hold values from 0.25 to 1.75
- w_qkv1: bfloat16 [512, 1536], P(None, 'lat'), may hold values from -0.25 to 0.25
- bias1: float32 [16, 20736], replicated, may hold values from -4 to 4
- w_out1: bfloat16 [512, 512], P(None, 'lat'), may hold values from -0.25 to 0.25
- gain_merge: float32 [2048], replicated, may hold values from 0.25 to 1.75
- w_merge: bfloat16 [2048, 1024], P(None, 'lat'), may hold values from -0.125 to 0.125
- gain2: float32 [1024], replicated, may hold values from 0.25 to 1.75
- w_qkv2: bfloat16 [1024, 3072], P(None, 'lat'), may hold values from -0.1875 to 0.1875
- bias2: float32 [32, 20736], replicated, may hold values from -4 to 4
- w_out2: bfloat16 [1024, 1024], P(None, 'lat'), may hold values from -0.1875 to 0.1875
Outputs:
- level_one: bfloat16 [768, 96, 2, 512], P('lat', 'lon')
- level_two: bfloat16 [384, 48, 2, 1024], P('lat', 'lon')
All inputs are finite; a program needn't handle non-finite values.
Results may differ from a plain program's by a relative error of at most 0.011.
Values may be sent and summed in bfloat16 or wider, within the bound.
A program may use at most 192 MiB of HBM per device.

v0:
```python
import jax
import jax.numpy as jnp
from jax import lax
from jax.sharding import PartitionSpec as P

HEAD = 32
WZ = 2
WL = 6
WN = 12
WT = 144


def passed_along(block, axis, distance):
    devices = range(lax.axis_size(axis))
    route = [((i - distance) % len(devices), i) for i in devices]
    return lax.ppermute(block, axis, route)


def from_behind(value, axis, steps):
    count = lax.axis_size(axis)
    initial, last = (max(0, -steps), min(count, count - steps))
    return lax.ppermute(value, axis, [(source, source + steps) for source in range(initial, last)])


def norm_rows(values, gain):
    mean = jnp.mean(values, -1, keepdims=True)
    centred = values - mean
    spread = jnp.mean(centred * centred, -1, keepdims=True)
    return centred * lax.rsqrt(spread + 1e-05) * gain


def window_attention(qkv, valid, bias, heads):
    rows, cols, levels, triple = qkv.shape
    width = triple // 3
    size = width // heads
    grid = qkv.reshape(rows // WL, WL, cols // WN, WN, levels // WZ, WZ, 3, heads, size)
    grid = grid.transpose(6, 0, 2, 4, 7, 1, 3, 5, 8).reshape(3, -1, heads, WT, size)
    scores = jnp.einsum(
        "whqd,whkd->whqk", grid[0], grid[1], preferred_element_type=jnp.float32
    ) / jnp.sqrt(jnp.float32(size))
    scores = scores + bias.reshape(heads, WT, WT)[None]
    keymask = jnp.repeat(valid.reshape(rows // WL, WL), WN * WZ, axis=1)
    keymask = jnp.repeat(keymask, cols // WN * (levels // WZ), axis=0)
    scores = jnp.where(keymask[:, None, None, :], scores, jnp.float32(-1e30))
    top = jnp.max(scores, -1, keepdims=True)
    weights = jnp.exp(scores - top)
    probs = (weights / jnp.sum(weights, -1, keepdims=True)).astype(jnp.bfloat16)
    mixed = jnp.einsum(
        "whqk,whkd->whqd", probs, grid[2], preferred_element_type=jnp.float32
    ).astype(jnp.bfloat16)
    mixed = mixed.reshape(rows // WL, cols // WN, levels // WZ, heads, WL, WN, WZ, size)
    return mixed.transpose(0, 4, 1, 5, 2, 6, 3, 7).reshape(rows, cols, levels, width)


def mixing(flat, weight, section):

    def column_block(piece):
        return jnp.dot(flat, piece, preferred_element_type=jnp.float32)

    if section == 0:
        return column_block(lax.all_gather(weight, "lat", axis=1, tiled=True))
    if section == 1:
        return column_block(lax.all_gather(weight, "lat", axis=1, tiled=True))
    if section == 2:
        return column_block(lax.all_gather(weight, "lat", axis=1, tiled=True))
    if section == 3:
        return column_block(lax.all_gather(weight, "lat", axis=1, tiled=True))
    return column_block(lax.all_gather(weight, "lat", axis=1, tiled=True))


def shifted_level(normed, project_qkv, bias, heads, level):
    lat_dev, lon_dev, levels, width = normed.shape
    half_lat = WL // 2
    half_lon = WN // 2
    lat_index = lax.axis_index("lat")
    lat_count = lax.axis_size("lat")
    if level == 1:
        beyond = passed_along(normed[:, :half_lon], "lon", -1)
    else:
        beyond = passed_along(normed[:, :half_lon], "lon", -1)
    widened = jnp.concatenate([normed[:, half_lon:], beyond], 1)
    if level == 1:
        below = from_behind(widened[:half_lat], "lat", -1)
    else:
        below = from_behind(widened[:half_lat], "lat", -1)
    padding = jnp.zeros((half_lat,) + widened.shape[1:], normed.dtype)
    padded = jnp.concatenate([padding, widened, below], 0)
    rows = padded.shape[0]
    qkv = (
        project_qkv(padded.reshape(-1, width))
        .astype(jnp.bfloat16)
        .reshape(rows, lon_dev, levels, 3 * width)
    )
    position = jnp.arange(rows, dtype=jnp.int32)
    valid = (position >= half_lat) & ((position < half_lat + lat_dev) | (lat_index < lat_count - 1))
    attended = window_attention(qkv, valid, bias, heads)
    if level == 1:
        returned = from_behind(attended[half_lat + lat_dev :], "lat", 1)
    else:
        returned = from_behind(attended[half_lat + lat_dev :], "lat", 1)
    leading = jnp.where(lat_index == 0, attended[half_lat : 2 * half_lat], returned)
    stacked = jnp.concatenate([leading, attended[2 * half_lat : half_lat + lat_dev]], 0)
    if level == 1:
        wrapped = passed_along(stacked[:, lon_dev - half_lon :], "lon", 1)
    else:
        wrapped = passed_along(stacked[:, lon_dev - half_lon :], "lon", 1)
    return jnp.concatenate([wrapped, stacked[:, : lon_dev - half_lon]], 1)


def attend_level(normed, project_qkv, bias, heads, level):
    return shifted_level(normed, project_qkv, bias, heads, level)


def shards(
    tokens,
    land_sea,
    surface_embed,
    level_table,
    level_embed,
    gain1,
    w_qkv1,
    bias1,
    w_out1,
    gain_merge,
    w_merge,
    gain2,
    w_qkv2,
    bias2,
    w_out2,
):
    lat_dev, lon_dev, levels, width = tokens.shape

    def product(flat, section, weight):
        return mixing(flat, weight, section)

    kinds = surface_embed.shape[0]
    surface_hot = (land_sea[..., None] == jnp.arange(kinds, dtype=jnp.int32)).astype(jnp.float32)
    surface = jnp.dot(
        surface_hot.reshape(-1, kinds), surface_embed, precision=lax.Precision.HIGHEST
    ).reshape(lat_dev, lon_dev, 1, width)
    level_hot = (level_table[:, None] == jnp.arange(level_embed.shape[0], dtype=jnp.int32)).astype(
        jnp.float32
    )
    level_rows = jnp.dot(level_hot, level_embed, precision=lax.Precision.HIGHEST)
    embedded = tokens.astype(jnp.float32) + surface + level_rows[None, None]
    normed1 = norm_rows(embedded, gain1).astype(jnp.bfloat16)
    attended1 = attend_level(
        normed1, lambda flat: product(flat, 0, w_qkv1), bias1, width // HEAD, 1
    )
    stream1 = embedded + product(attended1.reshape(-1, width), 1, w_out1).reshape(
        lat_dev, lon_dev, levels, width
    )
    level_one = stream1.astype(jnp.bfloat16)
    merged = jnp.concatenate(
        [stream1[0::2, 0::2], stream1[1::2, 0::2], stream1[0::2, 1::2], stream1[1::2, 1::2]], -1
    )
    mnormed = norm_rows(merged, gain_merge).astype(jnp.bfloat16)
    half_rows = lat_dev // 2
    half_cols = lon_dev // 2
    stream2 = product(mnormed.reshape(-1, 4 * width), 2, w_merge).reshape(
        half_rows, half_cols, levels, 2 * width
    )
    normed2 = norm_rows(stream2, gain2).astype(jnp.bfloat16)
    attended2 = attend_level(
        normed2, lambda flat: product(flat, 3, w_qkv2), bias2, 2 * width // HEAD, 2
    )
    level_two = stream2 + product(attended2.reshape(-1, 2 * width), 4, w_out2).reshape(
        half_rows, half_cols, levels, 2 * width
    )
    return (level_one, level_two.astype(jnp.bfloat16))


def solution(mesh):
    placed = (
        P("lat", "lon", None, None),
        P("lat", "lon"),
        P(),
        P(),
        P(),
        P(),
        P(None, "lat"),
        P(),
        P(None, "lat"),
        P(),
        P(None, "lat"),
        P(),
        P(None, "lat"),
        P(),
        P(None, "lat"),
    )
    return jax.shard_map(
        shards,
        mesh=mesh,
        in_specs=placed,
        out_specs=(P("lat", "lon", None, None), P("lat", "lon", None, None)),
        check_vma=False,
    )
```

profile of v0, /device:TPU:4, one launch (start us, length us, event | category | flops | bytes accessed | tf_op | source)
XLA Modules:
  0.0 1230.6 jit_solution(13708982383260640119)
XLA Ops:
  7.2 0.7 all-gather.5.cloned.1.call-update
  8.0 0.7 all-gather.7.cloned.1.call-update
  9.5 0.8 fusion.60
  10.3 1.2 fusion.53
  11.5 1.3 fusion.39
  13.8 3.0 collective-permute-done
  16.9 1.3 collective-permute-start.1
  18.4 3.2 add.79
  21.6 3.8 copy.37
  25.4 1.2 pad_maximum_fusion
  26.5 0.8 copy.33
  27.7 283.5 %all-gather.5.cloned.1.call-done = bf16[512,1536]{0,1:T(8,128)(2,1)} async-done(((bf16[512,24]{0,1:T(8,128)(2,1)}), bf16[512,1536]{0,1:T(8,128)(2,1)}) %all-gather.5.cloned.1.call-update) | async-done | bytes 1572880 | tf_op jit(solution)/shard_map/all_gather | solution.py:61
  311.2 4.5 convolution_convert_fusion.1
  315.7 12.3 reshape_reshape.6
  328.0 6.3 copy.86
  334.4 5.2 fusion.76
  339.6 5.1 fusion.17
  344.7 8.0 fusion.80
  352.7 9.5 fusion.26
  362.2 3.9 copy.40
  366.0 4.8 copy.41
  370.9 5.1 reshape.170
  376.0 2.6 collective-permute-start.2
  378.6 2.6 collective-permute-done.2
  381.4 160.3 %all_gather.16 = bf16[512,512]{0,1:T(8,128)(2,1)S(1)} all-gather(bf16[512,8]{0,1:T(8,128)(2,1)S(1)} %copy-done.8), channel_id=1, replica_groups=mesh['lat'=64,'lon'=4] {'lat'}, dimensions={1}, use_global_device_ids=true | all-gather | bytes 532480 | tf_op jit(solution)/shard_map/all_gather | solution.py:63
  544.1 70.6 %all-gather.7.cloned.1.call-done = bf16[2048,1024]{0,1:T(8,128)(2,1)} async-done(((bf16[2048,16]{0,1:T(8,128)(2,1)}), bf16[2048,1024]{0,1:T(8,128)(2,1)}) %all-gather.7.cloned.1.call-update) | async-done | bytes 4194320 | tf_op jit(solution)/shard_map/all_gather | solution.py:65
  614.6 3.8 fusion.82
  619.1 6.5 collective-permute-done.4
  625.6 1.3 collective-permute-start.5
  627.1 6.3 add.85
  633.4 6.2 copy.46
  640.7 280.9 %all-gather.9.cloned.1.call-done = bf16[1024,3072]{0,1:T(8,128)(2,1)} async-done(((bf16[1024,48]{0,1:T(8,128)(2,1)}), bf16[1024,3072]{0,1:T(8,128)(2,1)}) %all-gather.9.cloned.1.call-update) | async-done | bytes 6291472 | tf_op jit(solution)/shard_map/all_gather | solution.py:67
  921.6 4.8 convolution_convert_fusion
  926.4 6.6 reshape_reshape.7
  933.1 5.4 copy.87
  938.5 3.4 fusion.77
  941.9 5.3 fusion.21
  947.2 11.2 fusion.83
  958.4 6.0 fusion.29
  964.4 3.4 copy.49
  967.9 3.0 reshape.173
  970.9 1.5 fusion.78
  972.4 2.5 collective-permute-start.6
  974.9 3.2 collective-permute-done.6
  978.3 1.3 copy.53
  979.6 240.8 %all-gather.11.cloned.1.call-done = bf16[1024,1024]{0,1:T(8,128)(2,1)} async-done(((bf16[1024,16]{0,1:T(8,128)(2,1)}), bf16[1024,1024]{0,1:T(8,128)(2,1)}) %all-gather.11.cloned.1.call-update) | async-done | bytes 2097168 | tf_op jit(solution)/shard_map/all_gather | solution.py:68
  1220.4 2.4 fusion.35
  1222.8 1.0 copy.54
  (91 shorter events, 7.1 us)
Async XLA Ops:
  7.2 2.3 copy-start
  7.2 5.6 copy-start.3
  7.2 6.0 copy-start.10
  7.2 304.0 %all-gather.5.cloned.1.call-start = ((), (), s32[]{:S(2)}) async-start(), calls=%async_computation | async-start | bytes 1597440 | tf_op jit(solution)/shard_map/all_gather | solution.py:61
  7.9 606.7 %all-gather.7.cloned.1.call-start = ((), (), s32[]{:S(2)}) async-start(), calls=%async_computation.1 | async-start | bytes 4259840 | tf_op jit(solution)/shard_map/all_gather | solution.py:65
  8.7 912.9 %all-gather.9.cloned.1.call-start = ((), (), s32[]{:S(2)}) async-start(), calls=%async_computation.2 | async-start | bytes 6389760 | tf_op jit(solution)/shard_map/all_gather | solution.py:67
  9.4 1210.9 %all-gather.11.cloned.1.call-start = ((), (), s32[]{:S(2)}) async-start(), calls=%async_computation.3 | async-start | bytes 2129920 | tf_op jit(solution)/shard_map/all_gather | solution.py:68
  13.1 5.2 copy-start.7
  13.6 3.3 collective-permute-start
  16.9 8.5 collective-permute-start.1
  344.7 8.0 copy-start.2
  370.9 10.5 copy-start.8
  376.0 5.2 collective-permute-start.2
  381.3 160.4 %collective-permute-start.3 = (bf16[12,6,2,512]{3,1,2,0:T(8,128)(2,1)S(1)}, bf16[12,6,2,512]{3,1,2,0:T(8,128)(2,1)S(1)}, u32[]{:S(2)}, u32[]{:S(2)}) collective-permute-start(bf16[12,6,2,512]{3,1,2,0:T(8,128)(2,1)S(1)} %pad_maximum_fusion.5), channel_id=1, source_target_pairs={{3,0},{0,1},{1,2},{2,3},{7,4},{4,5},{5,6},{6,7},{11,8},{8,9},{9,10... | collective-permute-start | bytes 442376 | tf_op jit(solution)/shard_map/ppermute | solution.py:16
  542.7 71.9 %copy-start.11 = (f32[2048]{0:T(1024)S(1)}, f32[2048]{0:T(1024)}, u32[]{:S(2)}) copy-start(f32[2048]{0:T(1024)} %param.24) | copy-start | bytes 24580
  544.0 74.7 %copy-start.9 = (f32[1024]{0:T(1024)S(1)}, f32[1024]{0:T(1024)}, u32[]{:S(2)}) copy-start(f32[1024]{0:T(1024)} %param.26) | copy-start | bytes 12292
  618.4 15.0 %copy-start.4 = (f32[6,12,2,1024]{3,1,2,0:T(8,128)}, f32[6,12,2,1024]{3,1,2,0:T(8,128)S(1)}, u32[]{:S(2)}) copy-start(f32[6,12,2,1024]{3,1,2,0:T(8,128)S(1)} %get-tuple-element.20) | copy-start | bytes 1769476
  619.0 6.5 collective-permute-start.4
  625.6 14.0 %collective-permute-start.5 = (bf16[3,12,2,1024]{3,1,2,0:T(8,128)(2,1)S(1)}, bf16[3,12,2,1024]{3,1,2,0:T(8,128)(2,1)S(1)}, u32[]{:S(2)}, u32[]{:S(2)}) collective-permute-start(bf16[3,12,2,1024]{3,1,2,0:T(8,128)(2,1)S(1)} %pad_maximum_fusion.4), channel_id=1, source_target_pairs={{4,0},{8,4},{12,8},{16,12},{20,16},{24,20},{28,24},{32,28},{36,32}... | collective-permute-start | bytes 442376 | tf_op jit(solution)/shard_map/ppermute | solution.py:22
  938.5 8.7 slice-start
  941.8 5.3 slice-start.1
  947.2 11.3 copy-start.6
  970.9 249.5 %copy-start.5 = (f32[6,12,2,1024]{3,1,2,0:T(8,128)S(1)}, f32[6,12,2,1024]{3,1,2,0:T(8,128)}, u32[]{:S(2)}) copy-start(f32[6,12,2,1024]{3,1,2,0:T(8,128)} %copy-done.4) | copy-start | bytes 1769476
  972.4 5.7 collective-permute-start.6
  978.2 242.2 %collective-permute-start.7 = (bf16[6,6,2,1024]{3,1,2,0:T(8,128)(2,1)S(1)}, bf16[6,6,2,1024]{3,1,2,0:T(8,128)(2,1)S(1)}, u32[]{:S(2)}, u32[]{:S(2)}) collective-permute-start(bf16[6,6,2,1024]{3,1,2,0:T(8,128)(2,1)S(1)} %fusion.52), channel_id=1, source_target_pairs={{3,0},{0,1},{1,2},{2,3},{7,4},{4,5},{5,6},{6,7},{11,8},{8,9},{9,10... | collective-permute-start | bytes 442376 | tf_op jit(solution)/shard_map/ppermute | solution.py:16
  978.3 245.6 %copy-start.1 = (f32[13,512]{1,0:T(8,128)S(1)}, f32[13,512]{1,0:T(8,128)}, u32[]{:S(2)}) copy-start(f32[13,512]{1,0:T(8,128)} %param.19) | copy-start | bytes 79876
Sparse Core Ops, SparseCore 0:
  9.8 301.2 all-gather.4
  313.0 301.6 all-gather.6
  616.4 305.1 all-gather.8
  923.2 297.0 all-gather.10
where the time goes:
time: 1240 us; the launch traced here: 1230 us
  waiting for transfers between devices  893 us (72%)
  blocking collectives  160 us (13%)
  local copies, waits for them, and re-layouts  86.3 us (7%)
  matrix products  44.1 us (4%)
  other arithmetic  24.1 us (2%)
  between operations  14.6 us (1%)
    all_gather x4, waiting for transfers between devices, mixing(): return column_block(lax.all_gather(weight, 'lat', axis=1, tiled=True))  876 us
    all_gather x1, blocking collectives, mixing(): return column_block(lax.all_gather(weight, 'lat', axis=1, tiled=True))  160 us
    another operation x4, local copies, waits for them, and re-layouts, window_attention(): qkv.reshape(rows // WL, WL, cols // WN, WN, levels // WZ, WZ, 3, heads, s...  30.7 us
  transfers between devices with their start and end apart: 12, of which 8 were waited for; matrix products, arithmetic and copies ran while one was open for 12% of the time, Pallas kernels for 0%

commit v1 on v0

v1 whole, which is shorter than its diff:
```python
import functools

import jax
import jax.numpy as jnp
from jax import lax
from jax.experimental import pallas as pl
from jax.experimental.pallas import tpu as pltpu
from jax.sharding import PartitionSpec as P

HEAD = 32
WZ = 2
WL = 6
WN = 12
WT = 144
MESH = pl.DeviceIdType.MESH
GROUPS = ((32, 512), (16, 2048), (48, 1024), (16, 1024))
NG = len(GROUPS)
ZS, YS, XS, SS = 0, 7, 11, 19
SLOTS = 32


class Place:
    def __init__(self):
        lat = lax.axis_index("lat")
        lon = lax.axis_index("lon")
        self.lat, self.lon = lat, lon
        self.z = lat // 8
        self.xlo = (lat // 4) % 2
        self.y = lat % 4
        self.xhi = lon // 2
        self.core = lon % 2
        self.x = self.xhi * 2 + self.xlo

    def at(self, x=None, y=None, z=None, core=None):
        x = self.x if x is None else x
        y = self.y if y is None else y
        z = self.z if z is None else z
        core = self.core if core is None else core
        return ((z * 2 + x % 2) * 4 + y, (x // 2) * 2 + core)


class Gather:
    def __init__(self, place, shard, full, send, recv):
        self.p, self.shard, self.full, self.send, self.recv = place, shard, full, send, recv
        p = place
        self.up = p.at(y=(p.y + 1) % 4)
        self.down = p.at(y=(p.y + 3) % 4)
        self.east = p.at(x=(p.x + 1) % 4)
        self.west = p.at(x=(p.x + 3) % 4)
        self.twin = p.at(core=1 - p.core)
        self.partners = [p.at(z=(p.z + d) % 8) for d in range(1, 8)] + [
            self.up, self.down, self.east, self.west, self.twin]

    def copy(self, g, slot, src, dst, to):
        return pltpu.make_async_remote_copy(
            src_ref=src, dst_ref=dst, send_sem=self.send.at[g, slot], recv_sem=self.recv.at[g, slot],
            device_id=to, device_id_type=MESH)

    def move(self, g, slot, to, half, zs, line):
        part = self.full[g].at[half, zs, line]
        self.copy(g, slot, part, part, to).start()

    def landed(self, g, slot, half, zs, line):
        part = self.full[g].at[half, zs, line]
        self.copy(g, slot, part, part, self.twin).wait_recv()

    def line(self, xlo, dy):
        return xlo * 4 + (self.p.y + dy) % 4

    def start(self, g):
        p = self.p
        mine = self.full[g].at[p.core, p.z, self.line(p.xlo, 0)]
        for d in range(1, 8):
            self.copy(g, ZS + d - 1, self.shard[g].at[p.core], mine, p.at(z=(p.z + d) % 8)).start()

    def after_z(self, g):
        p = self.p
        own = self.line(p.xlo, 0)
        mine = self.full[g].at[p.core, p.z, own]
        for d in range(1, 8):
            part = self.full[g].at[p.core, (p.z + 8 - d) % 8, own]
            self.copy(g, ZS + d - 1, part, part, self.twin).wait_recv()
        whole = pl.ds(0, 8)
        self.move(g, YS + 0, self.up, p.core, whole, own)
        self.move(g, YS + 1, self.down, p.core, whole, own)
        self.to_x(g, 0, 0)
        self.to_x(g, 0, 1)
        self.move(g, SS + 0, self.twin, p.core, whole, own)

    def to_x(self, g, dy, part):
        p = self.p
        zs = pl.ds(4 * part, 4)
        self.move(g, XS + 2 * dy + part, (self.east, self.west)[part], p.core, zs, self.line(p.xlo, dy))

    def after_y(self, g):
        p = self.p
        whole = pl.ds(0, 8)
        below, above = self.line(p.xlo, 3), self.line(p.xlo, 1)
        self.landed(g, YS + 0, p.core, whole, below)
        self.move(g, YS + 2, self.up, p.core, pl.ds(0, 4), below)
        self.landed(g, YS + 1, p.core, whole, above)
        self.move(g, YS + 3, self.down, p.core, pl.ds(4, 4), above)
        for dy in (3, 1):
            for part in (0, 1):
                self.to_x(g, dy, part)
        self.move(g, SS + 1, self.twin, p.core, whole, below)
        self.move(g, SS + 2, self.twin, p.core, whole, above)

    def after_far(self, g):
        p = self.p
        far = self.line(p.xlo, 2)
        for part in (0, 1):
            zs = pl.ds(4 * part, 4)
            self.landed(g, YS + 2 + part, p.core, zs, far)
            self.to_x(g, 2, part)
            self.move(g, SS + 3 + part, self.twin, p.core, zs, far)

    def after_x(self, g):
        p = self.p
        for dy in (0, 3, 1, 2):
            for part in (0, 1):
                zs = pl.ds(4 * part, 4)
                line = self.line(1 - p.xlo, dy)
                self.landed(g, XS + 2 * dy + part, p.core, zs, line)
                self.move(g, SS + 5 + 2 * dy + part, self.twin, p.core, zs, line)

    def finish(self, g):
        p = self.p
        half = 1 - p.core
        whole = pl.ds(0, 8)
        self.landed(g, SS + 0, half, whole, self.line(p.xlo, 0))
        self.landed(g, SS + 1, half, whole, self.line(p.xlo, 3))
        self.landed(g, SS + 2, half, whole, self.line(p.xlo, 1))
        for part in (0, 1):
            zs = pl.ds(4 * part, 4)
            self.landed(g, SS + 3 + part, half, zs, self.line(p.xlo, 2))
            for dy in range(4):
                self.landed(g, SS + 5 + 2 * dy + part, half, zs, self.line(1 - p.xlo, dy))

    def drain(self, g):
        p = self.p

        def sent(slot, src):
            self.copy(g, slot, src, src, self.twin).wait_send()

        for d in range(1, 8):
            sent(ZS + d - 1, self.shard[g].at[p.core])
        whole = self.full[g].at[p.core, pl.ds(0, 8), 0]
        half = self.full[g].at[p.core, pl.ds(0, 4), 0]
        for slot in (YS, YS + 1, SS, SS + 1, SS + 2):
            sent(slot, whole)
        for slot in (YS + 2, YS + 3, SS + 3, SS + 4):
            sent(slot, half)
        for k in range(8):
            sent(XS + k, half)
            sent(SS + 5 + k, half)


def gather_kernel(*refs):
    shard, out = refs[:NG], refs[NG:2 * NG]
    full = refs[2 * NG:3 * NG]
    send, recv, local = refs[3 * NG:]
    place = Place()
    net = Gather(place, shard, full, send, recv)
    barrier = pltpu.get_barrier_semaphore()
    for to in net.partners:
        pl.semaphore_signal(barrier, inc=1, device_id=to, device_id_type=MESH)
    pl.semaphore_wait(barrier, len(net.partners))
    for g in range(NG):
        own = pltpu.make_async_copy(
            shard[g].at[place.core], full[g].at[place.core, place.z, net.line(place.xlo, 0)], local.at[g])
        own.start()
        net.start(g)
        own.wait()
    for step in range(NG + 4):
        for k, act in enumerate((net.after_z, net.after_y, net.after_far, net.after_x, net.finish)):
            g = step - k
            if 0 <= g < NG:
                act(g)
    for g in range(NG):
        pltpu.make_async_copy(full[g], out[g], local.at[g]).start()
    for g in range(NG):
        net.drain(g)
    for g in range(NG):
        pltpu.make_async_copy(full[g], out[g], local.at[g]).wait()


def gather_weights(w_qkv1, w_out1, w_merge, w_qkv2, w_out2):
    shards = [jnp.concatenate([w_qkv1, w_out1], 1), w_merge, w_qkv2, w_out2]
    shards = [w.T.reshape(w.shape[1], 2, w.shape[0] // 2).transpose(1, 0, 2) for w in shards]
    shapes = [(2, 8, 8, rows, depth // 2) for rows, depth in GROUPS]
    full = pl.pallas_call(
        gather_kernel,
        out_shape=[jax.ShapeDtypeStruct(s, jnp.bfloat16) for s in shapes],
        in_specs=[pl.BlockSpec(memory_space=pltpu.VMEM)] * NG,
        out_specs=[pl.BlockSpec(memory_space=pl.ANY)] * NG,
        scratch_shapes=[pltpu.VMEM(s, jnp.bfloat16) for s in shapes] + [
            pltpu.SemaphoreType.DMA((NG, SLOTS)),
            pltpu.SemaphoreType.DMA((NG, SLOTS)),
            pltpu.SemaphoreType.DMA((NG,)),
        ],
        compiler_params=pltpu.CompilerParams(
            collective_id=0, has_side_effects=True, vmem_limit_bytes=40 * 2**20),
    )(*shards)
    whole = [f.reshape(2, 64, rows, depth // 2) for f, (rows, depth) in zip(full, GROUPS)]

    def columns(f, first, last):
        return f[:, :, first:last].transpose(0, 3, 1, 2).reshape(-1, 64 * (last - first))

    return (
        columns(whole[0], 0, 24),
        columns(whole[0], 24, 32),
        columns(whole[1], 0, 16),
        columns(whole[2], 0, 48),
        columns(whole[3], 0, 16),
    )


def passed_along(block, axis, distance):
    devices = range(lax.axis_size(axis))
    route = [((i - distance) % len(devices), i) for i in devices]
    return lax.ppermute(block, axis, route)


def from_behind(value, axis, steps):
    count = lax.axis_size(axis)
    initial, last = (max(0, -steps), min(count, count - steps))
    return lax.ppermute(value, axis, [(source, source + steps) for source in range(initial, last)])


def norm_rows(values, gain):
    mean = jnp.mean(values, -1, keepdims=True)
    centred = values - mean
    spread = jnp.mean(centred * centred, -1, keepdims=True)
    return centred * lax.rsqrt(spread + 1e-05) * gain


def window_attention(qkv, valid, bias, heads):
    rows, cols, levels, triple = qkv.shape
    width = triple // 3
    size = width // heads
    grid = qkv.reshape(rows // WL, WL, cols // WN, WN, levels // WZ, WZ, 3, heads, size)
    grid = grid.transpose(6, 0, 2, 4, 7, 1, 3, 5, 8).reshape(3, -1, heads, WT, size)
    scores = jnp.einsum(
        "whqd,whkd->whqk", grid[0], grid[1], preferred_element_type=jnp.float32
    ) / jnp.sqrt(jnp.float32(size))
    scores = scores + bias.reshape(heads, WT, WT)[None]
    keymask = jnp.repeat(valid.reshape(rows // WL, WL), WN * WZ, axis=1)
    keymask = jnp.repeat(keymask, cols // WN * (levels // WZ), axis=0)
    scores = jnp.where(keymask[:, None, None, :], scores, jnp.float32(-1e30))
    top = jnp.max(scores, -1, keepdims=True)
    weights = jnp.exp(scores - top)
    probs = (weights / jnp.sum(weights, -1, keepdims=True)).astype(jnp.bfloat16)
    mixed = jnp.einsum(
        "whqk,whkd->whqd", probs, grid[2], preferred_element_type=jnp.float32
    ).astype(jnp.bfloat16)
    mixed = mixed.reshape(rows // WL, cols // WN, levels // WZ, heads, WL, WN, WZ, size)
    return mixed.transpose(0, 4, 1, 5, 2, 6, 3, 7).reshape(rows, cols, levels, width)


def shifted_level(normed, w_qkv, bias, heads):
    lat_dev, lon_dev, levels, width = normed.shape
    half_lat = WL // 2
    half_lon = WN // 2
    lat_index = lax.axis_index("lat")
    lat_count = lax.axis_size("lat")
    beyond = passed_along(normed[:, :half_lon], "lon", -1)
    widened = jnp.concatenate([normed[:, half_lon:], beyond], 1)
    below = from_behind(widened[:half_lat], "lat", -1)
    padding = jnp.zeros((half_lat,) + widened.shape[1:], normed.dtype)
    padded = jnp.concatenate([padding, widened, below], 0)
    rows = padded.shape[0]
    qkv = jnp.dot(padded.reshape(-1, width), w_qkv, preferred_element_type=jnp.float32)
    qkv = qkv.astype(jnp.bfloat16).reshape(rows, lon_dev, levels, 3 * width)
    position = jnp.arange(rows, dtype=jnp.int32)
    valid = (position >= half_lat) & ((position < half_lat + lat_dev) | (lat_index < lat_count - 1))
    attended = window_attention(qkv, valid, bias, heads)
    returned = from_behind(attended[half_lat + lat_dev :], "lat", 1)
    leading = jnp.where(lat_index == 0, attended[half_lat : 2 * half_lat], returned)
    stacked = jnp.concatenate([leading, attended[2 * half_lat : half_lat + lat_dev]], 0)
    wrapped = passed_along(stacked[:, lon_dev - half_lon :], "lon", 1)
    return jnp.concatenate([wrapped, stacked[:, : lon_dev - half_lon]], 1)


def shards(
    tokens, land_sea, surface_embed, level_table, level_embed, gain1, w_qkv1, bias1, w_out1,
    gain_merge, w_merge, gain2, w_qkv2, bias2, w_out2,
):
    lat_dev, lon_dev, levels, width = tokens.shape
    w_qkv1, w_out1, w_merge, w_qkv2, w_out2 = gather_weights(w_qkv1, w_out1, w_merge, w_qkv2, w_out2)

    def product(flat, weight):
        return jnp.dot(flat, weight, preferred_element_type=jnp.float32)

    kinds = surface_embed.shape[0]
    surface_hot = (land_sea[..., None] == jnp.arange(kinds, dtype=jnp.int32)).astype(jnp.float32)
    surface = jnp.dot(
        surface_hot.reshape(-1, kinds), surface_embed, precision=lax.Precision.HIGHEST
    ).reshape(lat_dev, lon_dev, 1, width)
    level_hot = (level_table[:, None] == jnp.arange(level_embed.shape[0], dtype=jnp.int32)).astype(
        jnp.float32
    )
    level_rows = jnp.dot(level_hot, level_embed, precision=lax.Precision.HIGHEST)
    embedded = tokens.astype(jnp.float32) + surface + level_rows[None, None]
    normed1 = norm_rows(embedded, gain1).astype(jnp.bfloat16)
    attended1 = shifted_level(normed1, w_qkv1, bias1, width // HEAD)
    stream1 = embedded + product(attended1.reshape(-1, width), w_out1).reshape(
        lat_dev, lon_dev, levels, width
    )
    level_one = stream1.astype(jnp.bfloat16)
    merged = jnp.concatenate(
        [stream1[0::2, 0::2], stream1[1::2, 0::2], stream1[0::2, 1::2], stream1[1::2, 1::2]], -1
    )
    mnormed = norm_rows(merged, gain_merge).astype(jnp.bfloat16)
    half_rows = lat_dev // 2
    half_cols = lon_dev // 2
    stream2 = product(mnormed.reshape(-1, 4 * width), w_merge).reshape(
        half_rows, half_cols, levels, 2 * width
    )
    normed2 = norm_rows(stream2, gain2).astype(jnp.bfloat16)
    attended2 = shifted_level(normed2, w_qkv2, bias2, 2 * width // HEAD)
    level_two = stream2 + product(attended2.reshape(-1, 2 * width), w_out2).reshape(
        half_rows, half_cols, levels, 2 * width
    )
    return (level_one, level_two.astype(jnp.bfloat16))


def solution(mesh):
    placed = (
        P("lat", "lon", None, None), P("lat", "lon"), P(), P(), P(), P(),
        P(None, "lat"), P(), P(None, "lat"), P(), P(None, "lat"), P(), P(None, "lat"), P(), P(None, "lat"),
    )
    return jax.shard_map(
        shards,
        mesh=mesh,
        in_specs=placed,
        out_specs=(P("lat", "lon", None, None), P("lat", "lon", None, None)),
        check_vma=False,
    )
```

time: 1240 us -> 320 us (0.26)
  the two profiles are of different devices: /device:TPU:4 before, /device:TPU:33 now
where the time goes in v1:
time: 320 us; the launch traced here: 316 us
  local copies, waits for them, and re-layouts  131 us (41%)
  Pallas kernels  66.5 us (21%)
  matrix products  43.7 us (14%)
  waiting for transfers between devices  27.6 us (9%)
  other arithmetic  27.5 us (9%)
  starting transfers between devices  18.6 us (6%)
    pallas_call x1, Pallas kernels, gather_weights(): pl.pallas_call(gather_kernel, out_shape=[jax.ShapeDtypeStruct(s, jnp.bflo...  66.5 us
    another operation x4, local copies, waits for them, and re-layouts, window_attention(): qkv.reshape(rows // WL, WL, cols // WN, WN, levels // WZ, WZ, 3, heads, s...  30.9 us
    reshape x3, local copies, waits for them, and re-layouts, gather_weights(): f.reshape(2, 64, rows, depth // 2)  25.8 us
    unnamed x77, local copies, waits for them, and re-layouts  19.3 us
    add x4, local copies, waits for them, and re-layouts, window_attention(): scores = scores + bias.reshape(heads, WT, WT)[None]  19.1 us
    sub x2, other arithmetic, window_attention(): weights = jnp.exp(scores - top)  19 us
    dot_general x2, matrix products, window_attention(): jnp.einsum('whqk,whkd->whqd', probs, grid[2], preferred_element_type=jnp....  15.4 us
    ppermute x4, waiting for transfers between devices, from_behind(): lax.ppermute(value, axis, [(source, source + steps) for source in range(i...  15.2 us
  transfers between devices with their start and end apart: 8, of which 4 were waited for; matrix products, arithmetic and copies ran while one was open for 19% of the time, Pallas kernels for 21%

profile of v1, /device:TPU:33, one launch (start us, length us, event | category | flops | bytes accessed | tf_op | source)
XLA Modules:
  0.0 316.3 jit_solution(10389466353545718479)
XLA Ops:
  2.2 1.2 fusion.53
  3.4 1.5 fusion.39
  4.9 1.4 multiply_reduce_fusion.1
  7.7 5.8 %collective-permute-done = bf16[12,6,2,512]{3,1,2,0:T(8,128)(2,1)S(1)} collective-permute-done((bf16[12,6,2,512]{3,1,2,0:T(8,128)(2,1)S(1)}, bf16[12,6,2,512]{3,1,2,0:T(8,128)(2,1)S(1)}, u32[]{:S(2)}, u32[]{:S(2)}) %collective-permute-start) | collective-permute-done | bytes 147488 | tf_op jit(solution)/shard_map/ppermute | solution.py:222
  13.6 5.2 %collective-permute-start.1 = (bf16[3,24,2,512]{3,1,2,0:T(8,128)(2,1)S(1)}, bf16[3,24,2,512]{3,1,2,0:T(8,128)(2,1)S(1)}, u32[]{:S(2)}, u32[]{:S(2)}) collective-permute-start(bf16[3,24,2,512]{3,1,2,0:T(8,128)(2,1)S(1)} %pad_maximum_fusion.6), channel_id=1, source_target_pairs={{4,0},{8,4},{12,8},{16,12},{20,16},{24,20},{28,24},{32,28},{36,32}... | collective-permute-start | bytes 442376 | tf_op jit(solution)/shard_map/ppermute | solution.py:228
  18.9 66.5 %shard_map.158 = (bf16[2,8,8,32,256]{4,3,2,1,0:T(8,128)(2,1)S(1)}, bf16[2,8,8,16,1024]{4,3,2,1,0:T(8,128)(2,1)S(1)}, bf16[2,8,8,48,512]{4,3,2,1,0:T(8,128)(2,1)}, bf16[2,8,8,16,512]{4,3,2,1,0:T(8,128)(2,1)S(1)}) custom-call(bf16[2,32,256]{2,1,0:T(8,128)(2,1)S(1)} %bitcast.125, bf16[2,16,1024]{2,1,0:T(8,128)(2,1)S(1)} %bitcast.124, ...), custom_call_target="tpu_custom_call" | custom-call | tf_op jit(solution)/shard_map/pallas_call | solution.py:192
  85.6 1.6 copy.78
  88.0 1.5 copy.87
  89.5 4.5 %add.79 = f32[16,144,144]{2,1,0:T(8,128)} reshape(f32[16,20736]{1,0:T(8,128)} %param.22) | data formatting | bytes 2654208 | tf_op jit(solution)/shard_map/add | solution.py:247
  94.1 3.5 %copy.45 = f32[16,144,144]{1,2,0:T(8,128)} copy(f32[16,144,144]{2,1,0:T(8,128)} %add.79) | data formatting | bytes 2654208 | tf_op jit(solution)/shard_map/add | solution.py:247
  98.9 1.3 reshape.244
  100.1 4.8 %convolution_convert_fusion.1 = bf16[864,1536]{1,0:T(8,128)(2,1)} fusion(bf16[864,512]{1,0:T(8,128)(2,1)} %reshape.244, bf16[512,1536]{0,1:T(8,128)(2,1)} %bitcast.151), kind=kOutput, calls=%fused_computation.29 | convolution fusion | flops 1360281600 | bytes 5111808 | tf_op jit(solution)/shard_map/dot_general | solution.py:273
  105.0 12.3 %reshape_reshape.6 = bf16[3,6,2,12,1,2,3,16,32]{8,7,6,5,3,2,1,0,4:T(8,128)(2,1)} reshape(bf16[864,1536]{1,0:T(8,128)(2,1)} %convolution_convert_fusion.1) | data formatting | bytes 5308416 | tf_op jit(solution)/shard_map/reshape;reshape | solution.py:242
  117.3 6.3 %copy.120 = bf16[3,6,2,12,1,2,3,16,32]{8,7,5,3,1,2,0,4,6:T(8,128)(2,1)S(1)} copy(bf16[3,6,2,12,1,2,3,16,32]{8,7,6,5,3,2,1,0,4:T(8,128)(2,1)} %reshape_reshape.6) | data formatting | bytes 5308416 | tf_op jit(solution)/shard_map/reshape;reshape | solution.py:242
  123.6 5.5 %fusion.76 = (bf16[1,3,2,1,16,6,12,2,32]{8,4,7,6,5,2,1,3,0:T(8,128)(2,1)}, bf16[1,3,2,1,16,6,12,2,32]{8,4,7,6,5,2,1,3,0:T(8,128)(2,1)}, bf16[1,3,2,1,16,6,12,2,32]{8,4,7,6,5,2,1,3,0:T(8,128)(2,1)}) fusion(bf16[3,3,2,1,16,6,12,2,32]{8,4,7,6,5,2,1,3,0:T(8,128)(2,1)S(1)} %bitcast.129), kind=kLoop, calls=%fused_computation.109 | loop fusion | bytes 5308416 | tf_op jit(solution)/shard_map/slice | solution.py:255
  129.1 5.1 %fusion.17 = f32[6,16,144,144]{2,3,1,0:T(8,128)S(1)} fusion(bf16[6,16,144,32]{3,1,2,0:T(8,128)(2,1)} %bitcast.134, bf16[6,16,144,32]{3,1,2,0:T(8,128)(2,1)} %bitcast.135), kind=kOutput, calls=%fused_computation.26 | convolution fusion | flops 127401984 | bytes 9732096 | tf_op jit(solution)/shard_map/whqd,whkd->whqk/dot_general | solution.py:244
  134.2 8.0 %fusion.80 = f32[6,16,144]{2,1,0:T(8,128)S(1)} fusion(f32[6,16,144,144]{2,3,1,0:T(8,128)S(1)} %fusion.17, f32[16,144,144]{1,2,0:T(8,128)} %copy.45, pred[6,144]{1,0:T(8,128)(4,1)S(1)} %broadcast_in_dim.63), kind=kOutput, calls=%fused_computation.113 | output fusion | flops 9953423 | bytes 9345888 | tf_op jit(solution)/shard_map/sub | solution.py:252
  142.2 10.4 %fusion.26 = bf16[6,16,144,32]{2,3,1,0:T(8,128)(2,1)} fusion(f32[6,16,144]{2,1,0:T(8,128)S(1)} %fusion.80, bf16[6,16,144,32]{3,1,2,0:T(8,128)(2,1)} %bitcast.146, f32[6,16,144,144]{2,3,1,0:T(8,128)} %copy-done.8, f32[16,144,144]{1,2,0:T(8,128)} %copy.45, pred[6,144]{1,0:T(8,128)(4,1)S(1)} %broadcast_in_dim.63), kind=kOutput, calls=%fused_computation.36 | convolution fusion | flops 139802256 | bytes 11115360 | tf_op jit(solution)/shard_map/whqk,whkd->whqd/dot_general | solution.py:254
  152.6 4.8 %copy.48 = bf16[6,16,144,32]{3,1,2,0:T(8,128)(2,1)} copy(bf16[6,16,144,32]{2,3,1,0:T(8,128)(2,1)} %fusion.26) | data formatting | bytes 1769472 | tf_op jit(solution)/shard_map/convert_element_type | solution.py:256
  157.4 4.8 %copy.49 = bf16[3,6,2,12,1,2,16,32]{7,6,3,2,5,1,0,4:T(8,128)(2,1)} copy(bf16[3,6,2,12,1,2,16,32]{7,6,5,3,1,2,0,4:T(8,128)(2,1)} %bitcast.133) | data formatting | bytes 1769472 | tf_op jit(solution)/shard_map/transpose | solution.py:258
  162.1 5.1 %reshape.252 = bf16[18,24,2,512]{3,1,2,0:T(8,128)(2,1)S(1)} reshape(bf16[3,6,2,12,1,2,16,32]{7,6,3,2,5,1,0,4:T(8,128)(2,1)} %copy.49) | data formatting | bytes 1769472 | tf_op jit(solution)/shard_map/reshape | solution.py:258
  167.3 1.9 collective-permute-start.2
  169.3 8.6 %collective-permute-done.2 = bf16[3,24,2,512]{3,1,2,0:T(8,128)(2,1)S(1)} collective-permute-done((bf16[3,24,2,512]{3,1,2,0:T(8,128)(2,1)S(1)}, bf16[3,24,2,512]{3,1,2,0:T(8,128)(2,1)S(1)}, u32[]{:S(2)}, u32[]{:S(2)}) %collective-permute-start.2) | collective-permute-done | bytes 147488 | tf_op jit(solution)/shard_map/ppermute | solution.py:228
  179.6 2.8 collective-permute-start.3
  183.1 6.3 %copy.52 = bf16[2,64,16,1024]{3,0,2,1:T(2,128)(2,1)} copy(bf16[2,64,16,1024]{3,2,1,0:T(8,128)(2,1)S(1)} %bitcast.119) | data formatting | bytes 8388608 | tf_op jit(solution)/shard_map/reshape | solution.py:205
  189.4 5.7 %copy.89 = bf16[128,8,2,1024]{3,1,2,0:T(8,128)(2,1)} copy(bf16[128,8,2,1024]{3,2,1,0:T(2,128)(2,1)} %bitcast.132) | data formatting | bytes 8388608
  195.1 1.3 fusion.81
  198.2 4.0 %fusion.82 = (f32[6,12,2]{1,2,0:T(2,128)S(1)}, f32[6,12,2,1024]{3,1,2,0:T(8,128)S(1)}) fusion(bf16[2048,1024]{0,1:T(8,128)(2,1)} %bitcast.145, f32[6,12,2,512]{3,1,2,0:T(8,128)S(1)} %slice.106, f32[6,12,2,512]{3,1,2,0:T(8,128)S(1)} %slice.105, f32[6,12,2,512]{3,1,2,0:T(8,128)S(1)} %slice.104, f32[6,12,2,512]{3,1,2,0:T(8,128)S(1)} %slice.103, ...), kind=kOutput, calls=%fused_computation.115 | convolution fusion | flops 606191488 | bytes 5973696 | tf_op jit(solution)/shard_map/dot_general | solution.py:293
  202.9 6.6 %collective-permute-done.4 = bf16[6,6,2,1024]{3,1,2,0:T(8,128)(2,1)S(1)} collective-permute-done((bf16[6,6,2,1024]{3,1,2,0:T(8,128)(2,1)S(1)}, bf16[6,6,2,1024]{3,1,2,0:T(8,128)(2,1)S(1)}, u32[]{:S(2)}, u32[]{:S(2)}) %collective-permute-start.4) | collective-permute-done | bytes 147488 | tf_op jit(solution)/shard_map/ppermute | solution.py:222
  210.2 2.1 collective-permute-start.5
  212.4 17.3 %copy.55 = bf16[2,64,48,512]{3,0,2,1:T(2,128)(2,1)S(1)} copy(bf16[2,64,48,512]{3,2,1,0:T(8,128)(2,1)S(1)} %bitcast.142) | data formatting | bytes 12582912 | tf_op jit(solution)/shard_map/reshape | solution.py:205
  229.7 4.7 %copy.90 = bf16[384,8,2,512]{3,1,2,0:T(8,128)(2,1)} copy(bf16[384,8,2,512]{3,2,1,0:T(2,128)(2,1)S(1)} %bitcast.131) | data formatting | bytes 12582912
  234.4 4.8 %add.85 = f32[32,144,144]{2,1,0:T(8,128)} reshape(f32[32,20736]{1,0:T(8,128)S(1)} %copy-done.14) | data formatting | bytes 5308416 | tf_op jit(solution)/shard_map/add | solution.py:247
  239.2 6.2 %copy.59 = f32[32,144,144]{1,2,0:T(8,128)} copy(f32[32,144,144]{2,1,0:T(8,128)} %add.85) | data formatting | bytes 5308416 | tf_op jit(solution)/shard_map/add | solution.py:247
  247.6 4.8 %convolution_convert_fusion = bf16[288,3072]{1,0:T(8,128)(2,1)S(1)} fusion(bf16[288,1024]{1,0:T(8,128)(2,1)S(1)} %reshape.256, bf16[1024,3072]{0,1:T(8,128)(2,1)} %bitcast.143), kind=kOutput, calls=%fused_computation.24 | convolution fusion | flops 1812824064 | bytes 8650752 | tf_op jit(solution)/shard_map/dot_general | solution.py:273
  252.5 6.9 %reshape_reshape.7 = bf16[2,6,1,12,1,2,3,32,32]{8,7,6,5,3,1,0,4,2:T(8,128)(2,1)} reshape(bf16[288,3072]{1,0:T(8,128)(2,1)S(1)} %convolution_convert_fusion) | data formatting | bytes 3538944 | tf_op jit(solution)/shard_map/reshape;reshape | solution.py:242
  259.3 5.4 %copy.121 = bf16[2,6,1,12,1,2,3,32,32]{8,7,5,3,1,0,4,2,6:T(8,128)(2,1)S(1)} copy(bf16[2,6,1,12,1,2,3,32,32]{8,7,6,5,3,1,0,4,2:T(8,128)(2,1)} %reshape_reshape.7) | data formatting | bytes 3538944 | tf_op jit(solution)/shard_map/reshape;reshape | solution.py:242
  264.7 3.3 %fusion.77 = (bf16[1,2,1,1,32,6,12,2,32]{8,4,7,6,5,1,3,2,0:T(8,128)(2,1)}, bf16[1,2,1,1,32,6,12,2,32]{8,4,7,6,5,1,3,2,0:T(8,128)(2,1)S(1)}, bf16[1,2,1,1,32,6,12,2,32]{8,4,7,6,5,1,3,2,0:T(8,128)(2,1)S(1)}) fusion(bf16[3,2,1,1,32,6,12,2,32]{8,4,7,6,5,1,3,2,0:T(8,128)(2,1)S(1)} %bitcast.130), kind=kLoop, calls=%fused_computation.110 | loop fusion | bytes 3538944 | tf_op jit(solution)/shard_map/slice | solution.py:255
  268.0 5.3 %fusion.21 = f32[2,32,144,144]{2,3,1,0:T(8,128)} fusion(bf16[2,32,144,32]{3,1,2,0:T(8,128)(2,1)S(1)} %bitcast.136, bf16[2,32,144,32]{3,1,2,0:T(8,128)(2,1)S(1)} %bitcast.137), kind=kOutput, calls=%fused_computation.31 | convolution fusion | flops 84934656 | bytes 6488064 | tf_op jit(solution)/shard_map/whqd,whkd->whqk/dot_general | solution.py:244
  273.3 11.0 %fusion.83 = (f32[2,32,144]{2,1,0:T(8,128)S(1)}, f32[2,32,144,144]{2,3,1,0:T(8,128)}) fusion(f32[2,32,144,144]{2,3,1,0:T(8,128)} %fusion.21, f32[32,144,144]{1,2,0:T(8,128)S(1)} %bitcast.128, pred[2,144]{1,0:T(4,128)(4,1)S(1)} %broadcast_in_dim.68), kind=kOutput, calls=%fused_computation.116 | output fusion | flops 10616975 | bytes 13308192 | tf_op jit(solution)/shard_map/sub | solution.py:252
  284.4 5.0 %fusion.29 = bf16[2,32,144,32]{2,3,1,0:T(8,128)(2,1)S(1)} fusion(f32[2,32,144,144]{2,3,1,0:T(8,128)} %get-tuple-element.30, f32[2,32,144]{2,1,0:T(8,128)S(1)} %get-tuple-element.29, bf16[2,32,144,32]{3,1,2,0:T(8,128)(2,1)S(1)} %bitcast.147), kind=kOutput, calls=%fused_computation.40 | convolution fusion | flops 87883776 | bytes 6524928 | tf_op jit(solution)/shard_map/whqk,whkd->whqd/dot_general | solution.py:254
  289.4 3.1 copy.62
  292.5 4.2 %reshape.260 = bf16[12,12,2,1024]{3,2,1,0:T(2,128)(2,1)S(1)} reshape(bf16[2,6,1,12,1,2,32,32]{7,6,5,3,1,0,4,2:T(8,128)(2,1)} %bitcast.138) | data formatting | bytes 1179648 | tf_op jit(solution)/shard_map/reshape | solution.py:258
  297.1 3.4 %collective-permute-start.6 = (bf16[3,12,2,1024]{3,1,2,0:T(8,128)(2,1)S(1)}, bf16[3,12,2,1024]{3,1,2,0:T(8,128)(2,1)S(1)}, u32[]{:S(2)}, u32[]{:S(2)}) collective-permute-start(bf16[3,12,2,1024]{3,1,2,0:T(8,128)(2,1)S(1)} %copy.81), channel_id=1, source_target_pairs={{0,4},{4,8},{8,12},{12,16},{16,20},{20,24},{24,28},{28,32},{32,36}... | collective-permute-start | bytes 442376 | tf_op jit(solution)/shard_map/ppermute | solution.py:228
  300.6 6.5 %collective-permute-done.6 = bf16[3,12,2,1024]{3,1,2,0:T(8,128)(2,1)S(1)} collective-permute-done((bf16[3,12,2,1024]{3,1,2,0:T(8,128)(2,1)S(1)}, bf16[3,12,2,1024]{3,1,2,0:T(8,128)(2,1)S(1)}, u32[]{:S(2)}, u32[]{:S(2)}) %collective-permute-start.6) | collective-permute-done | bytes 147488 | tf_op jit(solution)/shard_map/ppermute | solution.py:228
  307.2 2.4 collective-permute-start.7
  309.6 2.2 copy.66
  312.9 1.3 copy.68
  (135 shorter events, 16.3 us)
Async XLA Ops:
  0.6 0.8 copy-start
  0.6 5.7 %copy-start.9 = (bf16[12,24,2,512]{3,2,1,0:T(2,128)(2,1)S(1)}, bf16[12,24,2,512]{3,2,1,0:T(2,128)(2,1)}, u32[]{:S(2)}) copy-start(bf16[12,24,2,512]{3,2,1,0:T(2,128)(2,1)} %param.15) | copy-start | bytes 1769476
  0.7 5.7 %copy-start.27 = (f32[512]{0:T(512)S(1)}, f32[512]{0:T(512)}, u32[]{:S(2)}) copy-start(f32[512]{0:T(512)} %param.20) | copy-start | bytes 6148
  3.4 4.3 %copy-start.6 = (f32[12,24,512]{2,1,0:T(8,128)}, f32[12,24,512]{2,1,0:T(8,128)S(1)}, u32[]{:S(2)}) copy-start(f32[12,24,512]{2,1,0:T(8,128)S(1)} %fusion.53) | copy-start | bytes 1769476
  6.3 12.5 %copy-start.24 = (bf16[512,24]{0,1:T(8,128)(2,1)S(1)}, bf16[512,24]{0,1:T(8,128)(2,1)}, u32[]{:S(2)}) copy-start(bf16[512,24]{0,1:T(8,128)(2,1)} %param.21) | copy-start | bytes 73732
  6.3 12.5 %copy-start.25 = (bf16[512,8]{0,1:T(8,128)(2,1)S(1)}, bf16[512,8]{0,1:T(8,128)(2,1)}, u32[]{:S(2)}) copy-start(bf16[512,8]{0,1:T(8,128)(2,1)} %param.23) | copy-start | bytes 24580
  6.3 12.5 %copy-start.22 = (bf16[2048,16]{0,1:T(8,128)(2,1)S(1)}, bf16[2048,16]{0,1:T(8,128)(2,1)}, u32[]{:S(2)}) copy-start(bf16[2048,16]{0,1:T(8,128)(2,1)} %param.25) | copy-start | bytes 196612
  6.4 12.5 %copy-start.21 = (bf16[1024,48]{0,1:T(8,128)(2,1)S(1)}, bf16[1024,48]{0,1:T(8,128)(2,1)}, u32[]{:S(2)}) copy-start(bf16[1024,48]{0,1:T(8,128)(2,1)} %param.27) | copy-start | bytes 294916
  6.4 12.5 %copy-start.23 = (bf16[1024,16]{0,1:T(8,128)(2,1)S(1)}, bf16[1024,16]{0,1:T(8,128)(2,1)}, u32[]{:S(2)}) copy-start(bf16[1024,16]{0,1:T(8,128)(2,1)} %param.29) | copy-start | bytes 98308
  6.8 6.7 %collective-permute-start = (bf16[12,6,2,512]{3,1,2,0:T(8,128)(2,1)S(1)}, bf16[12,6,2,512]{3,1,2,0:T(8,128)(2,1)S(1)}, u32[]{:S(2)}, u32[]{:S(2)}) collective-permute-start(bf16[12,6,2,512]{3,1,2,0:T(8,128)(2,1)S(1)} %slice.119), channel_id=1, source_target_pairs={{1,0},{2,1},{3,2},{0,3},{5,4},{6,5},{7,6},{4,7},{9,8},{10,9},{11,1... | collective-permute-start | bytes 442376 | tf_op jit(solution)/shard_map/ppermute | solution.py:222
  13.6 84.2 %collective-permute-start.1 = (bf16[3,24,2,512]{3,1,2,0:T(8,128)(2,1)S(1)}, bf16[3,24,2,512]{3,1,2,0:T(8,128)(2,1)S(1)}, u32[]{:S(2)}, u32[]{:S(2)}) collective-permute-start(bf16[3,24,2,512]{3,1,2,0:T(8,128)(2,1)S(1)} %pad_maximum_fusion.6), channel_id=1, source_target_pairs={{4,0},{8,4},{12,8},{16,12},{20,16},{24,20},{28,24},{32,28},{36,32}... | collective-permute-start | bytes 442376 | tf_op jit(solution)/shard_map/ppermute | solution.py:228
  85.4 2.0 copy-start.2
  85.4 2.6 copy-start.4
  134.2 8.0 %copy-start.8 = (f32[6,16,144,144]{2,3,1,0:T(8,128)}, f32[6,16,144,144]{2,3,1,0:T(8,128)S(1)}, u32[]{:S(2)}) copy-start(f32[6,16,144,144]{2,3,1,0:T(8,128)S(1)} %fusion.17) | copy-start | bytes 23887876
  167.2 2.0 copy-start.13
  167.3 10.6 %collective-permute-start.2 = (bf16[3,24,2,512]{3,1,2,0:T(8,128)(2,1)S(1)}, bf16[3,24,2,512]{3,1,2,0:T(8,128)(2,1)S(1)}, u32[]{:S(2)}, u32[]{:S(2)}) collective-permute-start(bf16[3,24,2,512]{3,1,2,0:T(8,128)(2,1)S(1)} %slice.125), channel_id=1, source_target_pairs={{0,4},{4,8},{8,12},{12,16},{16,20},{20,24},{24,28},{28,32},{32,36}... | collective-permute-start | bytes 442376 | tf_op jit(solution)/shard_map/ppermute | solution.py:228
  169.2 9.6 %copy-start.11 = (bf16[9,24,2,512]{3,1,2,0:T(8,128)(2,1)}, bf16[9,24,2,512]{3,1,2,0:T(8,128)(2,1)S(1)}, u32[]{:S(2)}) copy-start(bf16[9,24,2,512]{3,1,2,0:T(8,128)(2,1)S(1)} %slice.126) | copy-start | bytes 1327108
  169.3 13.8 %copy-start.3 = (bf16[2,8,8,16,1024]{4,3,2,1,0:T(8,128)(2,1)S(1)}, bf16[2,8,8,16,1024]{4,3,2,1,0:T(8,128)(2,1)}, u32[]{:S(2)}) copy-start(bf16[2,8,8,16,1024]{4,3,2,1,0:T(8,128)(2,1)} %copy-done.2) | copy-start | bytes 12582916
  179.6 15.5 %collective-permute-start.3 = (bf16[12,6,2,512]{3,1,2,0:T(8,128)(2,1)}, bf16[12,6,2,512]{3,1,2,0:T(8,128)(2,1)S(1)}, u32[]{:S(2)}, u32[]{:S(2)}) collective-permute-start(bf16[12,6,2,512]{3,1,2,0:T(8,128)(2,1)} %pad_maximum_fusion.5), channel_id=1, source_target_pairs={{3,0},{0,1},{1,2},{2,3},{7,4},{4,5},{5,6},{6,7},{11,8},{8,9},{9,10... | collective-permute-start | bytes 442376 | tf_op jit(solution)/shard_map/ppermute | solution.py:222
  189.4 5.7 %copy-start.7 = (f32[12,24,512]{2,1,0:T(8,128)S(1)}, f32[12,24,512]{2,1,0:T(8,128)}, u32[]{:S(2)}) copy-start(f32[12,24,512]{2,1,0:T(8,128)} %copy-done.6) | copy-start | bytes 1769476
  189.4 5.7 %copy-start.10 = (bf16[12,24,2,512]{3,2,1,0:T(2,128)(2,1)S(1)}, bf16[12,24,2,512]{3,2,1,0:T(2,128)(2,1)}, u32[]{:S(2)}) copy-start(bf16[12,24,2,512]{3,2,1,0:T(2,128)(2,1)} %param.15) | copy-start | bytes 1769476
  189.4 5.7 %copy-start.12 = (bf16[9,24,2,512]{3,1,2,0:T(8,128)(2,1)S(1)}, bf16[9,24,2,512]{3,1,2,0:T(8,128)(2,1)}, u32[]{:S(2)}) copy-start(bf16[9,24,2,512]{3,1,2,0:T(8,128)(2,1)} %copy-done.11) | copy-start | bytes 1327108
  196.9 1.4 copy-start.28
  198.2 14.1 %slice-start.2 = ((s8[6291456]{0:T(1024)(128)(4,1)}), s8[4194304]{0:T(1024)(128)(4,1)S(1)}, s32[]{:S(2)}) async-start(s8[6291456]{0:T(1024)(128)(4,1)} %bitcast.140), calls=%async_computation.2 | async-start | bytes 8388608
  198.2 4.3 %copy-start.26 = (f32[1024]{0:T(1024)S(1)}, f32[1024]{0:T(1024)}, u32[]{:S(2)}) copy-start(f32[1024]{0:T(1024)} %param.26) | copy-start | bytes 12292
  198.2 14.1 %slice-start.3 = ((s8[6291456]{0:T(1024)(128)(4,1)}), s8[2097152]{0:T(1024)(128)(4,1)S(1)}, s32[]{:S(2)}) async-start(s8[6291456]{0:T(1024)(128)(4,1)} %bitcast.140), calls=%async_computation.3 | async-start | bytes 4194304
  202.8 9.6 %copy-start.17 = (bf16[6,6,2,1024]{3,1,2,0:T(8,128)(2,1)}, bf16[6,6,2,1024]{3,1,2,0:T(8,128)(2,1)S(1)}, u32[]{:S(2)}) copy-start(bf16[6,6,2,1024]{3,1,2,0:T(8,128)(2,1)S(1)} %get-tuple-element.23) | copy-start | bytes 442372
  202.8 6.7 %collective-permute-start.4 = (bf16[6,6,2,1024]{3,1,2,0:T(8,128)(2,1)S(1)}, bf16[6,6,2,1024]{3,1,2,0:T(8,128)(2,1)S(1)}, u32[]{:S(2)}, u32[]{:S(2)}) collective-permute-start(bf16[6,6,2,1024]{3,1,2,0:T(8,128)(2,1)S(1)} %get-tuple-element.24), channel_id=1, source_target_pairs={{1,0},{2,1},{3,2},{0,3},{5,4},{6,5},{7,6},{4,7},{9,8},{10,9},{11,1... | collective-permute-start | bytes 442376 | tf_op jit(solution)/shard_map/ppermute | solution.py:222
  209.4 2.9 copy-start.19
  210.2 35.4 %collective-permute-start.5 = (bf16[3,12,2,1024]{3,1,2,0:T(8,128)(2,1)}, bf16[3,12,2,1024]{3,1,2,0:T(8,128)(2,1)}, u32[]{:S(2)}, u32[]{:S(2)}) collective-permute-start(bf16[3,12,2,1024]{3,1,2,0:T(8,128)(2,1)} %pad_maximum_fusion.4), channel_id=1, source_target_pairs={{4,0},{8,4},{12,8},{16,12},{20,16},{24,20},{28,24},{32,28},{36,32}... | collective-permute-start | bytes 442376 | tf_op jit(solution)/shard_map/ppermute | solution.py:228
  229.7 4.7 %copy-start.14 = (f32[32,20736]{1,0:T(8,128)S(1)}, f32[32,20736]{1,0:T(8,128)}, u32[]{:S(2)}) copy-start(f32[32,20736]{1,0:T(8,128)} %param.28) | copy-start | bytes 7962628
  239.2 6.4 %copy-start.18 = (bf16[6,6,2,1024]{3,1,2,0:T(8,128)(2,1)S(1)}, bf16[6,6,2,1024]{3,1,2,0:T(8,128)(2,1)}, u32[]{:S(2)}) copy-start(bf16[6,6,2,1024]{3,1,2,0:T(8,128)(2,1)} %copy-done.17) | copy-start | bytes 442372
  239.2 6.4 %copy-start.20 = (bf16[6,6,2,1024]{3,1,2,0:T(8,128)(2,1)S(1)}, bf16[6,6,2,1024]{3,1,2,0:T(8,128)(2,1)}, u32[]{:S(2)}) copy-start(bf16[6,6,2,1024]{3,1,2,0:T(8,128)(2,1)} %copy-done.19) | copy-start | bytes 442372
  264.7 8.6 %slice-start = ((s8[4718592]{0:T(1024)(128)(4,1)}), s8[4194304]{0:T(1024)(128)(4,1)S(1)}, s32[]{:S(2)}) async-start(s8[4718592]{0:T(1024)(128)(4,1)} %bitcast.127), calls=%async_computation | async-start | bytes 8388608
  268.0 5.3 %slice-start.1 = ((s8[4718592]{0:T(1024)(128)(4,1)}), s8[524288]{0:T(1024)(128)(4,1)S(1)}, s32[]{:S(2)}) async-start(s8[4718592]{0:T(1024)(128)(4,1)} %bitcast.127), calls=%async_computation.1 | async-start | bytes 1048576
  273.3 11.0 %copy-start.16 = (bf16[1,2,1,1,32,6,12,2,32]{8,4,7,6,5,1,3,2,0:T(8,128)(2,1)S(1)}, bf16[1,2,1,1,32,6,12,2,32]{8,4,7,6,5,1,3,2,0:T(8,128)(2,1)}, u32[]{:S(2)}) copy-start(bf16[1,2,1,1,32,6,12,2,32]{8,4,7,6,5,1,3,2,0:T(8,128)(2,1)} %get-tuple-element.17) | copy-start | bytes 1769476
  292.5 17.1 %copy-start.5 = (bf16[2,8,8,16,512]{4,3,2,1,0:T(8,128)(2,1)S(1)}, bf16[2,8,8,16,512]{4,3,2,1,0:T(8,128)(2,1)}, u32[]{:S(2)}) copy-start(bf16[2,8,8,16,512]{4,3,2,1,0:T(8,128)(2,1)} %copy-done.4) | copy-start | bytes 6291460
  297.1 10.0 %collective-permute-start.6 = (bf16[3,12,2,1024]{3,1,2,0:T(8,128)(2,1)S(1)}, bf16[3,12,2,1024]{3,1,2,0:T(8,128)(2,1)S(1)}, u32[]{:S(2)}, u32[]{:S(2)}) collective-permute-start(bf16[3,12,2,1024]{3,1,2,0:T(8,128)(2,1)S(1)} %copy.81), channel_id=1, source_target_pairs={{0,4},{4,8},{8,12},{12,16},{16,20},{20,24},{24,28},{28,32},{32,36}... | collective-permute-start | bytes 442376 | tf_op jit(solution)/shard_map/ppermute | solution.py:228
  307.2 6.9 %collective-permute-start.7 = (bf16[6,6,2,1024]{3,1,2,0:T(8,128)(2,1)S(1)}, bf16[6,6,2,1024]{3,1,2,0:T(8,128)(2,1)S(1)}, u32[]{:S(2)}, u32[]{:S(2)}) collective-permute-start(bf16[6,6,2,1024]{3,1,2,0:T(8,128)(2,1)S(1)} %fusion.52), channel_id=1, source_target_pairs={{3,0},{0,1},{1,2},{2,3},{7,4},{4,5},{5,6},{6,7},{11,8},{8,9},{9,10... | collective-permute-start | bytes 442376 | tf_op jit(solution)/shard_map/ppermute | solution.py:222
  311.8 1.1 copy-start.15
  314.2 1.9 copy-start.1

commit v2 on v1

v2 whole, which is shorter than its diff:
```python
import jax
import jax.numpy as jnp
from jax import lax
from jax.experimental import pallas as pl
from jax.experimental.pallas import tpu as pltpu
from jax.sharding import PartitionSpec as P

WT = 144
NT = (((1,), (1,)), ((), ()))
LOG2E = 1.4426950408889634
ABSENT = -1e30
MESH = pl.DeviceIdType.MESH
GROUPS = ((32, 512), (16, 2048), (48, 1024), (16, 1024))
NG = len(GROUPS)
ZS, YS, XS, SS = 0, 7, 11, 19
SLOTS = 32


class Place:
    def __init__(self):
        lat = lax.axis_index("lat")
        lon = lax.axis_index("lon")
        self.lat, self.lon = lat, lon
        self.z = lat // 8
        self.xlo = (lat // 4) % 2
        self.y = lat % 4
        self.xhi = lon // 2
        self.core = lon % 2
        self.x = self.xhi * 2 + self.xlo

    def at(self, x=None, y=None, z=None, core=None):
        x = self.x if x is None else x
        y = self.y if y is None else y
        z = self.z if z is None else z
        core = self.core if core is None else core
        return ((z * 2 + x % 2) * 4 + y, (x // 2) * 2 + core)


class Gather:
    def __init__(self, place, shard, full, send, recv):
        self.p, self.shard, self.full, self.send, self.recv = place, shard, full, send, recv
        p = place
        self.up = p.at(y=(p.y + 1) % 4)
        self.down = p.at(y=(p.y + 3) % 4)
        self.east = p.at(x=(p.x + 1) % 4)
        self.west = p.at(x=(p.x + 3) % 4)
        self.twin = p.at(core=1 - p.core)
        self.partners = [p.at(z=(p.z + d) % 8) for d in range(1, 8)] + [
            self.up, self.down, self.east, self.west, self.twin]

    def copy(self, g, slot, src, dst, to):
        return pltpu.make_async_remote_copy(
            src_ref=src, dst_ref=dst, send_sem=self.send.at[g, slot], recv_sem=self.recv.at[g, slot],
            device_id=to, device_id_type=MESH)

    def move(self, g, slot, to, half, zs, line):
        part = self.full[g].at[half, zs, line]
        self.copy(g, slot, part, part, to).start()

    def landed(self, g, slot, half, zs, line):
        part = self.full[g].at[half, zs, line]
        self.copy(g, slot, part, part, self.twin).wait_recv()

    def line(self, xlo, dy):
        return xlo * 4 + (self.p.y + dy) % 4

    def start(self, g):
        p = self.p
        mine = self.full[g].at[p.core, p.z, self.line(p.xlo, 0)]
        for d in range(1, 8):
            self.copy(g, ZS + d - 1, self.shard[g].at[p.core], mine, p.at(z=(p.z + d) % 8)).start()

    def after_z(self, g):
        p = self.p
        own = self.line(p.xlo, 0)
        mine = self.full[g].at[p.core, p.z, own]
        for d in range(1, 8):
            part = self.full[g].at[p.core, (p.z + 8 - d) % 8, own]
            self.copy(g, ZS + d - 1, part, part, self.twin).wait_recv()
        whole = pl.ds(0, 8)
        self.move(g, YS + 0, self.up, p.core, whole, own)
        self.move(g, YS + 1, self.down, p.core, whole, own)
        self.to_x(g, 0, 0)
        self.to_x(g, 0, 1)
        self.move(g, SS + 0, self.twin, p.core, whole, own)

    def to_x(self, g, dy, part):
        p = self.p
        zs = pl.ds(4 * part, 4)
        self.move(g, XS + 2 * dy + part, (self.east, self.west)[part], p.core, zs, self.line(p.xlo, dy))

    def after_y(self, g):
        p = self.p
        whole = pl.ds(0, 8)
        below, above = self.line(p.xlo, 3), self.line(p.xlo, 1)
        self.landed(g, YS + 0, p.core, whole, below)
        self.move(g, YS + 2, self.up, p.core, pl.ds(0, 4), below)
        self.landed(g, YS + 1, p.core, whole, above)
        self.move(g, YS + 3, self.down, p.core, pl.ds(4, 4), above)
        for dy in (3, 1):
            for part in (0, 1):
                self.to_x(g, dy, part)
        self.move(g, SS + 1, self.twin, p.core, whole, below)
        self.move(g, SS + 2, self.twin, p.core, whole, above)

    def after_far(self, g):
        p = self.p
        far = self.line(p.xlo, 2)
        for part in (0, 1):
            zs = pl.ds(4 * part, 4)
            self.landed(g, YS + 2 + part, p.core, zs, far)
            self.to_x(g, 2, part)
            self.move(g, SS + 3 + part, self.twin, p.core, zs, far)

    def after_x(self, g):
        p = self.p
        for dy in (0, 3, 1, 2):
            for part in (0, 1):
                zs = pl.ds(4 * part, 4)
                line = self.line(1 - p.xlo, dy)
                self.landed(g, XS + 2 * dy + part, p.core, zs, line)
                self.move(g, SS + 5 + 2 * dy + part, self.twin, p.core, zs, line)

    def finish(self, g):
        p = self.p
        half = 1 - p.core
        whole = pl.ds(0, 8)
        self.landed(g, SS + 0, half, whole, self.line(p.xlo, 0))
        self.landed(g, SS + 1, half, whole, self.line(p.xlo, 3))
        self.landed(g, SS + 2, half, whole, self.line(p.xlo, 1))
        for part in (0, 1):
            zs = pl.ds(4 * part, 4)
            self.landed(g, SS + 3 + part, half, zs, self.line(p.xlo, 2))
            for dy in range(4):
                self.landed(g, SS + 5 + 2 * dy + part, half, zs, self.line(1 - p.xlo, dy))

    def drain(self, g):
        p = self.p

        def sent(slot, src):
            self.copy(g, slot, src, src, self.twin).wait_send()

        for d in range(1, 8):
            sent(ZS + d - 1, self.shard[g].at[p.core])
        whole = self.full[g].at[p.core, pl.ds(0, 8), 0]
        half = self.full[g].at[p.core, pl.ds(0, 4), 0]
        for slot in (YS, YS + 1, SS, SS + 1, SS + 2):
            sent(slot, whole)
        for slot in (YS + 2, YS + 3, SS + 3, SS + 4):
            sent(slot, half)
        for k in range(8):
            sent(XS + k, half)
            sent(SS + 5 + k, half)


def times(a, b):
    return lax.dot_general(a, b, NT, preferred_element_type=jnp.float32)


def norm_groups(parts, gain):
    width = 128 * len(parts)
    mean = jnp.sum(sum(parts), -1, keepdims=True) / width
    parts = [p - mean for p in parts]
    spread = jnp.sum(sum(p * p for p in parts), -1, keepdims=True) / width
    scale = lax.rsqrt(spread + 1e-05)
    return [p * scale * gain[:, 128 * k:128 * k + 128] for k, p in enumerate(parts)]


def prepare_bias(flat, table, heads):
    lane = lax.broadcasted_iota(jnp.int32, (8, 128), 1)

    def eight(i, _):
        t, q = i // 18, i % 18
        rows = pl.ds(pl.multiple_of(t * 8, 8), 8)
        block = flat[rows, pl.ds(pl.multiple_of(q * 1152, 128), 1152)] * LOG2E
        for s in range(8):
            first, second = block[:, 128 * s:128 * s + 128], block[:, 128 * s + 128:128 * s + 256]
            if s:
                first, second = pltpu.roll(first, 128 - 16 * s, 1), pltpu.roll(second, 128 - 16 * s, 1)
                first = jnp.where(lane < 128 - 16 * s, first, second)
            second = jnp.where(lane < 16, second, ABSENT)
            where = pl.ds(t * 8 * WT + q * 8 + s, 8, stride=WT)
            table[0, where, :] = first
            table[1, where, :] = second
        return 0

    lax.fori_loop(0, heads // 8 * 18, eight, 0)


def attend(q, k, v, bias0, bias1, mask):
    lane = lax.broadcasted_iota(jnp.int32, (WT, 128), 1) // 32
    none = jnp.zeros((256 - WT, 128), jnp.bfloat16)
    heads = jnp.concatenate([jnp.where(lane == h, q, jnp.zeros_like(q)) for h in range(4)], 0)
    scores = times(heads, jnp.concatenate([k, none], 0)) * (LOG2E / 32 ** 0.5)
    bias = jnp.concatenate([bias0, bias1], 1)
    scores = scores + bias + jnp.concatenate([mask] * 4, 0)
    top = jnp.max(scores, -1, keepdims=True)
    weights = jnp.exp2(scores - top).astype(jnp.bfloat16)
    values = jnp.concatenate([jnp.concatenate([v, none], 0), jnp.ones((256, 128), jnp.bfloat16)], 1)
    mixed = jnp.dot(weights, values, preferred_element_type=jnp.float32)
    total, over = mixed[:WT, :128], mixed[:WT, 128:]
    for h in range(1, 4):
        total = jnp.where(lane == h, mixed[WT * h:WT * h + WT, :128], total)
        over = jnp.where(lane == h, mixed[WT * h:WT * h + WT, 128:], over)
    return total / over


def loop(count, step, first=0):
    lax.fori_loop(first, count, lambda i, c: (step(i), c)[1], 0)


def block_kernel(
    shard0, shard1, shard2, shard3, emb, gain1, gain_merge, gain2, bias1_hbm, bias2_hbm,
    one, two,
    full0, full1, full2, full3, flat1, flat2, table1, table2, mask,
    e1, first1, south1, rw1, rn1, rc1, bw1, bn1, bc1, qw, ow, x1, qkv1, s1, mg, mn,
    s2, e2, first2, south2, rw2, rn2, rc2, bw2, bn2, bc2, x2, qkv2,
    sw1, sn1, sc1, sw2, sn2, sc2,
    send, recv, hsend, hrecv, local,
):
    p = Place()
    full = (full0, full1, full2, full3)
    net = Gather(p, (shard0, shard1, shard2, shard3), full, send, recv)
    north, south = (p.lat + 63) % 64, (p.lat + 1) % 64
    west, east = (p.lon + 3) % 4, (p.lon + 1) % 4
    around = [(p.lat, west), (north, p.lon), (north, west), (p.lat, east), (south, p.lon), (south, east)]
    partners = net.partners + around
    barrier = pltpu.get_barrier_semaphore()
    for to in partners:
        pl.semaphore_signal(barrier, inc=1, device_id=to, device_id_type=MESH)
    b1 = pltpu.make_async_copy(bias1_hbm, flat1, local.at[0])
    b2 = pltpu.make_async_copy(bias2_hbm, flat2, local.at[1])
    b1.start()
    b2.start()
    pl.semaphore_wait(barrier, len(partners))

    def neighbour(slot, src, dst, way):
        return pltpu.make_async_remote_copy(
            src_ref=src, dst_ref=dst, send_sem=hsend.at[slot], recv_sem=hrecv.at[slot],
            device_id=around[way], device_id_type=MESH)

    owns = []
    for g in range(NG):
        own = pltpu.make_async_copy(
            net.shard[g].at[p.core], full[g].at[p.core, p.z, net.line(p.xlo, 0)], local.at[2 + g])
        own.start()
        owns.append(own)
    net.start(0)

    sixteen = lax.broadcasted_iota(jnp.int32, (16, 512), 0)
    sixteen2 = lax.broadcasted_iota(jnp.int32, (16, 1024), 0)

    def row_norm(r):
        v = emb[pl.ds(pl.multiple_of(r * 48, 16), 48), :]
        n = norm_groups([v[:, 128 * k:128 * k + 128] for k in range(4)], gain1[...])
        e1[r, 0:8, :] = jnp.zeros((8, 512), jnp.float32)
        e1[r, 48:64, :] = jnp.zeros((16, 512), jnp.float32)
        for k in range(4):
            e1[r, 4:52, 128 * k:128 * k + 128] = n[k]
        first1[r] = e1[r, 0:16, :].astype(jnp.bfloat16)

    loop(12, row_norm)
    for r in range(3):
        south1[r] = e1[r, 16:64, :].astype(jnp.bfloat16)
    halo1 = [neighbour(0, first1.at[pl.ds(3, 9)], rw1, 0), neighbour(1, south1, rn1, 1),
             neighbour(2, first1.at[pl.ds(0, 3)], rc1, 2)]
    for c in halo1:
        c.start()
    for own in owns:
        own.wait()
    net.after_z(0)
    net.start(1)

    half = lambda axis: lax.broadcasted_iota(jnp.int32, (WT, 256), axis) >= WT // 2
    cut = (half(0) != half(1)) & (p.lat == 63)
    mask[0] = jnp.zeros((WT, 256), jnp.float32)
    mask[1] = jnp.where(cut, ABSENT, 0.0)
    b1.wait()
    prepare_bias(flat1, table1, 16)
    net.after_y(0)
    net.after_z(1)
    net.start(2)
    net.after_far(0)
    net.after_y(1)
    b2.wait()
    prepare_bias(flat2, table2, 32)
    net.after_x(0)
    net.after_z(2)
    net.start(3)
    net.after_far(1)

    for c in halo1:
        c.wait_recv()

    def take_west(r):
        e1[r + 3, 48:64, :] = jnp.where(sixteen >= 4, rw1[r].astype(jnp.float32), e1[r + 3, 48:64, :])

    loop(9, take_west)
    for r in range(3):
        n = rn1[r].astype(jnp.float32)
        e1[12 + r, 16:48, :] = n[:32]
        e1[12 + r, 48:64, :] = jnp.where(sixteen >= 4, rc1[r].astype(jnp.float32), n[32:])
    for w in range(4):
        a, b = w // 2, w % 2
        x1[WT * w:WT * w + WT, :] = e1[3 + 6 * a:9 + 6 * a, 16 + 24 * b:40 + 24 * b, :].reshape(
            WT, 512).astype(jnp.bfloat16)

    net.finish(0)

    def unpack(i):
        z, l = i // 4, 2 * (i % 4)
        both = [jnp.concatenate([full0[0, z, l + d], full0[1, z, l + d]], 1).astype(jnp.float32)
                for d in range(2)]
        qw[pl.ds(pl.multiple_of(48 * i, 16), 48), :] = jnp.concatenate(
            [both[0][:24], both[1][:24]], 0).astype(jnp.bfloat16)
        ow[pl.ds(pl.multiple_of(16 * i, 16), 16), :] = jnp.concatenate(
            [both[0][24:], both[1][24:]], 0).astype(jnp.bfloat16)

    loop(32, unpack)

    def project1(n):
        out = times(x1[...], qw[pl.ds(pl.multiple_of(256 * n, 256), 256), :]).astype(jnp.bfloat16)
        qkv1[2 * n] = out[:, :128]
        qkv1[2 * n + 1] = out[:, 128:]

    loop(6, project1)
    net.after_x(1)
    net.after_y(2)
    net.after_z(3)

    def attend1(i):
        w, g = 3 - i // 4, i % 4
        rows = pl.ds(pl.multiple_of(WT * w, 16), WT)
        heads = pl.ds(pl.multiple_of(4 * WT * g, 16), 4 * WT)
        out = attend(qkv1[g, rows, :], qkv1[4 + g, rows, :], qkv1[8 + g, rows, :],
                     table1[0, heads, :], table1[1, heads, :], mask[w // 2])
        e1[pl.ds(3 + 6 * (w // 2), 6), pl.ds(pl.multiple_of(16 + 24 * (w % 2), 8), 24),
           pl.ds(pl.multiple_of(128 * g, 128), 128)] = out.reshape(6, 24, 128)

    loop(8, attend1)
    for r in range(3):
        bn1[r] = e1[12 + r, 16:64, :].astype(jnp.bfloat16)
        bc1[r] = e1[12 + r, 48:64, :].astype(jnp.bfloat16)
    back1 = [neighbour(3, bn1, sn1, 4), neighbour(4, bc1, sc1, 5)]
    for c in back1:
        c.start()
    net.after_far(2)
    net.after_y(3)
    loop(12, attend1, 8)

    def last_columns(r):
        bw1[r] = e1[r + 3, 48:64, :].astype(jnp.bfloat16)

    loop(9, last_columns)
    back1.append(neighbour(5, bw1, sw1, 3))
    back1[2].start()
    net.after_x(2)
    loop(16, attend1, 12)
    net.after_far(3)
    net.finish(1)
    for c in back1:
        c.wait_recv()

    def keep_west(r):
        e1[r + 3, 0:16, :] = jnp.where(sixteen >= 4, sw1[r].astype(jnp.float32), e1[r + 3, 0:16, :])

    loop(9, keep_west)
    for r in range(3):
        e1[r, 16:64, :] = sn1[r].astype(jnp.float32)
        e1[r, 0:16, :] = sc1[r].astype(jnp.float32)

    def collect1(r):
        x1[pl.ds(pl.multiple_of(48 * r, 16), 48), :] = e1[r, 4:52, :].astype(jnp.bfloat16)

    loop(12, collect1)
    for n in range(2):
        cols = slice(256 * n, 256 * n + 256)
        out = emb[:, cols] + times(x1[...], ow[cols, :])
        one[:, cols] = out.astype(jnp.bfloat16)
        s1[2 * n] = out[:, :128]
        s1[2 * n + 1] = out[:, 128:]

    def merge_rows(i):
        for dr in range(2):
            for dc in range(2):
                for level in range(2):
                    for k in range(4):
                        mg[(dc * 2 + dr) * 4 + k, pl.ds(24 * i + level, 12, stride=2), :] = s1[
                            k, pl.ds((2 * i + dr) * 48 + 2 * dc + level, 12, stride=4), :]

    loop(6, merge_rows)

    def merge_norm(c):
        rows = pl.ds(pl.multiple_of(16 * c, 16), 16)
        n = norm_groups([mg[k, rows, :] for k in range(16)], gain_merge[...])
        for k in range(16):
            mn[rows, 128 * k:128 * k + 128] = n[k].astype(jnp.bfloat16)

    loop(9, merge_norm)

    def merge_product(n):
        zs = pl.ds(2 * n, 2)
        out = times(mn[:, :1024], full1[0, zs].reshape(256, 1024))
        out = out + times(mn[:, 1024:], full1[1, zs].reshape(256, 1024))
        s2[2 * n] = out[:, :128]
        s2[2 * n + 1] = out[:, 128:]

    loop(4, merge_product)
    net.after_x(3)

    def row_norm2(r):
        rows = pl.ds(pl.multiple_of(24 * r, 8), 24)
        n = norm_groups([s2[k, rows, :] for k in range(8)], gain2[...])
        e2[r, 0:8, :] = jnp.zeros((8, 1024), jnp.float32)
        e2[r, 24:40, :] = jnp.zeros((16, 1024), jnp.float32)
        for k in range(8):
            e2[r, 4:28, 128 * k:128 * k + 128] = n[k]
        first2[r] = e2[r, 0:16, :].astype(jnp.bfloat16)
        south2[r] = e2[r, 16:32, :].astype(jnp.bfloat16)

    loop(6, row_norm2)
    halo2 = [neighbour(6, first2.at[pl.ds(3, 3)], rw2, 0), neighbour(7, south2.at[pl.ds(0, 3)], rn2, 1),
             neighbour(8, first2.at[pl.ds(0, 3)], rc2, 2)]
    for c in halo2:
        c.start()
    net.finish(2)
    for c in halo2:
        c.wait_recv()
    for r in range(3):
        e2[3 + r, 24:40, :] = jnp.where(sixteen2 >= 4, rw2[r].astype(jnp.float32), e2[3 + r, 24:40, :])
        e2[6 + r, 16:32, :] = rn2[r].astype(jnp.float32)
        e2[6 + r, 24:40, :] = jnp.where(sixteen2 >= 4, rc2[r].astype(jnp.float32), e2[6 + r, 24:40, :])
    x2[...] = e2[3:9, 16:40, :].reshape(WT, 1024).astype(jnp.bfloat16)

    def project2(z):
        out = times(x2[:, :512], full2[0, z].reshape(384, 512))
        out = (out + times(x2[:, 512:], full2[1, z].reshape(384, 512))).astype(jnp.bfloat16)
        for k in range(3):
            qkv2[3 * z + k] = out[:, 128 * k:128 * k + 128]

    loop(8, project2)

    def attend2(g):
        heads = pl.ds(pl.multiple_of(4 * WT * g, 16), 4 * WT)
        out = attend(qkv2[g], qkv2[8 + g], qkv2[16 + g], table2[0, heads, :], table2[1, heads, :], mask[1])
        e2[3:9, 16:40, pl.ds(pl.multiple_of(128 * g, 128), 128)] = out.reshape(6, 24, 128)

    loop(8, attend2)
    for r in range(3):
        bw2[r] = e2[3 + r, 24:40, :].astype(jnp.bfloat16)
        bn2[r] = e2[6 + r, 16:32, :].astype(jnp.bfloat16)
        bc2[r] = e2[6 + r, 24:40, :].astype(jnp.bfloat16)
    back2 = [neighbour(9, bw2, sw2, 3), neighbour(10, bn2, sn2, 4), neighbour(11, bc2, sc2, 5)]
    for c in back2:
        c.start()
    net.finish(3)
    for c in back2:
        c.wait_recv()
    for r in range(3):
        e2[3 + r, 0:16, :] = jnp.where(sixteen2 >= 4, sw2[r].astype(jnp.float32), e2[3 + r, 0:16, :])
        e2[r, 16:32, :] = sn2[r].astype(jnp.float32)
        e2[r, 0:16, :] = sc2[r].astype(jnp.float32)
    for r in range(6):
        x2[24 * r:24 * r + 24, :] = e2[r, 4:28, :].astype(jnp.bfloat16)

    def last(n):
        zs = pl.ds(2 * n, 2)
        out = times(x2[:, :512], full3[0, zs].reshape(256, 512))
        out = out + times(x2[:, 512:], full3[1, zs].reshape(256, 512))
        out = out + jnp.concatenate([s2[2 * n], s2[2 * n + 1]], 1)
        two[:, pl.ds(pl.multiple_of(256 * n, 256), 256)] = out.astype(jnp.bfloat16)

    loop(4, last)
    for c in halo1 + back1 + halo2 + back2:
        c.wait_send()
    for g in range(NG):
        net.drain(g)


def shards(
    tokens, land_sea, surface_embed, level_table, level_embed, gain1, w_qkv1, bias1, w_out1,
    gain_merge, w_merge, gain2, w_qkv2, bias2, w_out2,
):
    weights = [jnp.concatenate([w_qkv1, w_out1], 1), w_merge, w_qkv2, w_out2]
    weights = [w.T.reshape(w.shape[1], 2, w.shape[0] // 2).transpose(1, 0, 2) for w in weights]
    kind = land_sea[:, :, None, None]
    surface = jnp.where(kind == 0, surface_embed[0], jnp.where(kind == 1, surface_embed[1], surface_embed[2]))
    numbers = jnp.arange(level_embed.shape[0], dtype=jnp.int32)
    level_rows = jnp.sum(
        jnp.where((level_table[:, None] == numbers)[:, :, None], level_embed[None], 0.0), 1)
    embedded = tokens.astype(jnp.float32) + surface + level_rows[None, None]
    f32, bf16 = jnp.float32, jnp.bfloat16
    shapes = [(2, 8, 8, rows, depth // 2) for rows, depth in GROUPS]
    scratch = [pltpu.VMEM(s, bf16) for s in shapes] + [pltpu.VMEM(s, t) for s, t in (
        ((16, WT * WT), f32), ((32, WT * WT), f32),
        ((2, 16 * WT, 128), f32), ((2, 32 * WT, 128), f32), ((2, WT, 256), f32),
        ((15, 64, 512), f32), ((12, 16, 512), bf16), ((3, 48, 512), bf16),
        ((9, 16, 512), bf16), ((3, 48, 512), bf16), ((3, 16, 512), bf16),
        ((9, 16, 512), bf16), ((3, 48, 512), bf16), ((3, 16, 512), bf16),
        ((1536, 512), bf16), ((512, 512), bf16), ((576, 512), bf16), ((12, 576, 128), bf16),
        ((4, 576, 128), f32), ((16, WT, 128), f32), ((WT, 2048), bf16),
        ((8, WT, 128), f32), ((9, 40, 1024), f32), ((6, 16, 1024), bf16), ((6, 16, 1024), bf16),
        ((3, 16, 1024), bf16), ((3, 16, 1024), bf16), ((3, 16, 1024), bf16),
        ((3, 16, 1024), bf16), ((3, 16, 1024), bf16), ((3, 16, 1024), bf16),
        ((WT, 1024), bf16), ((24, WT, 128), bf16),
        ((9, 16, 512), bf16), ((3, 48, 512), bf16), ((3, 16, 512), bf16),
        ((3, 16, 1024), bf16), ((3, 16, 1024), bf16), ((3, 16, 1024), bf16),
    )] + [
        pltpu.SemaphoreType.DMA((NG, SLOTS)), pltpu.SemaphoreType.DMA((NG, SLOTS)),
        pltpu.SemaphoreType.DMA((12,)), pltpu.SemaphoreType.DMA((12,)), pltpu.SemaphoreType.DMA((6,)),
    ]
    vmem, anywhere = pl.BlockSpec(memory_space=pltpu.VMEM), pl.BlockSpec(memory_space=pl.ANY)
    one, two = pl.pallas_call(
        block_kernel,
        out_shape=[jax.ShapeDtypeStruct((576, 512), bf16), jax.ShapeDtypeStruct((WT, 1024), bf16)],
        in_specs=[vmem] * 8 + [anywhere] * 2,
        out_specs=[vmem] * 2,
        scratch_shapes=scratch,
        compiler_params=pltpu.CompilerParams(
            collective_id=0, has_side_effects=True, vmem_limit_bytes=60 * 2**20),
    )(*weights, embedded.reshape(576, 512), gain1[None], gain_merge[None], gain2[None], bias1, bias2)
    return one.reshape(12, 24, 2, 512), two.reshape(6, 12, 2, 1024)


def solution(mesh):
    placed = (
        P("lat", "lon", None, None), P("lat", "lon"), P(), P(), P(), P(),
        P(None, "lat"), P(), P(None, "lat"), P(), P(None, "lat"), P(), P(None, "lat"), P(), P(None, "lat"),
    )
    return jax.shard_map(
        shards,
        mesh=mesh,
        in_specs=placed,
        out_specs=(P("lat", "lon", None, None), P("lat", "lon", None, None)),
        check_vma=False,
    )
```

time: 320 us -> 117 us (0.37)
  the two profiles are of different devices: /device:TPU:33 before, /device:TPU:1 now
where the time goes in v2:
time: 117 us
  Pallas kernels  103 us (88%)
  local copies, waits for them, and re-layouts  8.63 us (7%)
  other arithmetic  4.1 us (4%)
    pallas_call x1, Pallas kernels, shards(): pl.pallas_call(block_kernel, out_shape=[jax.ShapeDtypeStruct((576, 512),...  103 us
    reshape x2, local copies, waits for them, and re-layouts, shards(): return (one.reshape(12, 24, 2, 512), two.reshape(6, 12, 2, 1024))  3.43 us
    reshape x4, local copies, waits for them, and re-layouts, shards(): w.T.reshape(w.shape[1], 2, w.shape[0] // 2).transpose(1, 0, 2)  2.51 us

profile of v2, /device:TPU:1, one launch (start us, length us, event | category | flops | bytes accessed | tf_op | source)
XLA Modules:
  0.0 116.6 jit_solution(11920800347803103244)
XLA Ops:
  0.6 0.8 fusion
  1.4 0.7 broadcast_compare_fusion.1
  2.1 0.1 select_select_fusion
  2.3 0.7 iota_compare_fusion
  3.0 0.9 select_reduce_fusion
  3.8 1.7 %add_add_fusion = f32[12,24,2,512]{3,2,1,0:T(2,128)S(1)} fusion(bf16[12,24,2,512]{3,2,1,0:T(2,128)(2,1)} %param.15, f32[2,512]{1,0:T(2,128)S(1)} %select_reduce_fusion, f32[12,24,512]{2,1,0:T(8,128)S(1)} %select_select_fusion), kind=kLoop, calls=%fused_computation | loop fusion | flops 884736 | bytes 2363392 | tf_op jit(solution)/shard_map/add | solution.py:491
  5.6 0.0 copy-start.1
  5.6 0.0 copy-start.2
  5.6 0.0 copy-start.4
  5.6 0.0 copy-start.5
  5.6 0.0 copy-start.3
  5.6 1.8 %reshape.64.emb = f32[576,512]{1,0:T(8,128)} reshape(f32[12,24,2,512]{3,2,1,0:T(2,128)S(1)} %add_add_fusion) | data formatting | bytes 2359296 | tf_op jit(solution)/shard_map/reshape | solution.py:521
  7.5 0.0 copy-done.1
  7.5 0.6 copy.33
  8.1 0.0 copy-done.2
  8.1 0.6 copy.34
  8.7 0.0 copy-done.4
  8.7 0.0 copy-done.5
  8.8 0.6 copy.36
  9.4 0.0 copy-done.3
  9.4 0.6 copy.35
  10.0 103.1 %shard_map.158 = (bf16[576,512]{1,0:T(8,128)(2,1)}, bf16[144,1024]{1,0:T(8,128)(2,1)}) custom-call(bf16[2,32,256]{2,1,0:T(8,128)(2,1)} %bitcast.40, bf16[2,16,1024]{2,1,0:T(8,128)(2,1)} %bitcast.39, bf16[2,48,512]{2,1,0:T(8,128)(2,1)} %bitcast.38, bf16[2,16,512]{2,1,0:T(8,128)(2,1)} %bitcast.41, f32[576,512]{1,0:T(8,128)} %reshape.64.emb, ...), custom_call_target="tpu_custom_call" | custom-call | tf_op jit(solution)/shard_map/pallas_call | solution.py:513
  113.1 0.0 copy-start
  113.1 2.6 %reshape.65 = bf16[12,24,2,512]{3,2,1,0:T(2,128)(2,1)} reshape(bf16[576,512]{1,0:T(8,128)(2,1)} %get-tuple-element.4) | data formatting | bytes 1179648 | tf_op jit(solution)/shard_map/reshape | solution.py:522
  115.7 0.0 copy-done
  115.7 0.8 reshape.66
  (1 shorter events, 0.0 us)
Async XLA Ops:
  5.6 1.9 %copy-start.1 = (bf16[1024,48]{0,1:T(8,128)(2,1)S(1)}, bf16[1024,48]{0,1:T(8,128)(2,1)}, u32[]{:S(2)}) copy-start(bf16[1024,48]{0,1:T(8,128)(2,1)} %param.27) | copy-start | bytes 294916
  5.6 2.5 %copy-start.2 = (bf16[2048,16]{0,1:T(8,128)(2,1)S(1)}, bf16[2048,16]{0,1:T(8,128)(2,1)}, u32[]{:S(2)}) copy-start(bf16[2048,16]{0,1:T(8,128)(2,1)} %param.25) | copy-start | bytes 196612
  5.6 3.2 %copy-start.4 = (bf16[512,24]{0,1:T(8,128)(2,1)S(1)}, bf16[512,24]{0,1:T(8,128)(2,1)}, u32[]{:S(2)}) copy-start(bf16[512,24]{0,1:T(8,128)(2,1)} %param.21) | copy-start | bytes 73732
  5.6 3.2 %copy-start.5 = (bf16[512,8]{0,1:T(8,128)(2,1)S(1)}, bf16[512,8]{0,1:T(8,128)(2,1)}, u32[]{:S(2)}) copy-start(bf16[512,8]{0,1:T(8,128)(2,1)} %param.23) | copy-start | bytes 24580
  5.6 3.8 %copy-start.3 = (bf16[1024,16]{0,1:T(8,128)(2,1)S(1)}, bf16[1024,16]{0,1:T(8,128)(2,1)}, u32[]{:S(2)}) copy-start(bf16[1024,16]{0,1:T(8,128)(2,1)} %param.29) | copy-start | bytes 98308
  113.1 2.6 %copy-start = (bf16[144,1024]{1,0:T(8,128)(2,1)S(1)}, bf16[144,1024]{1,0:T(8,128)(2,1)}, u32[]{:S(2)}) copy-start(bf16[144,1024]{1,0:T(8,128)(2,1)} %get-tuple-element.5) | copy-start | bytes 884740

commit v3 on v2

--- a/solution.py
+++ b/solution.py
@@ -12,8 +12,8 @@
 MESH = pl.DeviceIdType.MESH
 GROUPS = ((32, 512), (16, 2048), (48, 1024), (16, 1024))
 NG = len(GROUPS)
-ZS, YS, XS, SS = 0, 7, 11, 19
-SLOTS = 32
+ZS, YS, XS, SS = 0, 7, 15, 23
+SLOTS = 36
 
 
 class Place:
@@ -37,120 +37,187 @@
 
 
 class Gather:
-    def __init__(self, place, shard, full, send, recv):
-        self.p, self.shard, self.full, self.send, self.recv = place, shard, full, send, recv
+    def __init__(self, place, g, full, send, recv):
         p = place
+        self.p, self.g, self.full, self.send, self.recv = p, g, full, send, recv
         self.up = p.at(y=(p.y + 1) % 4)
         self.down = p.at(y=(p.y + 3) % 4)
         self.east = p.at(x=(p.x + 1) % 4)
         self.west = p.at(x=(p.x + 3) % 4)
         self.twin = p.at(core=1 - p.core)
         self.partners = [p.at(z=(p.z + d) % 8) for d in range(1, 8)] + [
-            self.up, self.down, self.east, self.west, self.twin]
-
-    def copy(self, g, slot, src, dst, to):
+            self.up, self.down, self.east, self.west, self.twin, p.at(y=(p.y + 2) % 4)]
+        self.sent = []
+
+    def copy(self, slot, part, to):
         return pltpu.make_async_remote_copy(
-            src_ref=src, dst_ref=dst, send_sem=self.send.at[g, slot], recv_sem=self.recv.at[g, slot],
-            device_id=to, device_id_type=MESH)
-
-    def move(self, g, slot, to, half, zs, line):
-        part = self.full[g].at[half, zs, line]
-        self.copy(g, slot, part, part, to).start()
-
-    def landed(self, g, slot, half, zs, line):
-        part = self.full[g].at[half, zs, line]
-        self.copy(g, slot, part, part, self.twin).wait_recv()
-
-    def line(self, xlo, dy):
+            src_ref=part, dst_ref=part, send_sem=self.send.at[self.g, slot],
+            recv_sem=self.recv.at[self.g, slot], device_id=to, device_id_type=MESH)
+
+    def part(self, half, zs, line):
+        return self.full.at[half, zs, line]
+
+    def move(self, slot, to, zs, line):
+        c = self.copy(slot, self.part(self.p.core, zs, line), to)
+        c.start()
+        self.sent.append(c)
+
+    def landed(self, slot, zs, line, half=None):
+        self.copy(slot, self.part(self.p.core if half is None else half, zs, line), self.twin).wait_recv()
+
+    def line(self, other, dy):
+        xlo = 1 - self.p.xlo if other else self.p.xlo
         return xlo * 4 + (self.p.y + dy) % 4
 
-    def start(self, g):
+    def drain(self):
+        for c in self.sent:
+            c.wait_send()
+
+    whole = pl.ds(0, 8)
+    parts = (pl.ds(0, 4), pl.ds(4, 4))
+
+    def start(self):
         p = self.p
-        mine = self.full[g].at[p.core, p.z, self.line(p.xlo, 0)]
         for d in range(1, 8):
-            self.copy(g, ZS + d - 1, self.shard[g].at[p.core], mine, p.at(z=(p.z + d) % 8)).start()
-
-    def after_z(self, g):
+            self.move(ZS + d - 1, p.at(z=(p.z + d) % 8), p.z, self.line(0, 0))
+
+    def z_landed(self):
         p = self.p
-        own = self.line(p.xlo, 0)
-        mine = self.full[g].at[p.core, p.z, own]
         for d in range(1, 8):
-            part = self.full[g].at[p.core, (p.z + 8 - d) % 8, own]
-            self.copy(g, ZS + d - 1, part, part, self.twin).wait_recv()
-        whole = pl.ds(0, 8)
-        self.move(g, YS + 0, self.up, p.core, whole, own)
-        self.move(g, YS + 1, self.down, p.core, whole, own)
-        self.to_x(g, 0, 0)
-        self.to_x(g, 0, 1)
-        self.move(g, SS + 0, self.twin, p.core, whole, own)
-
-    def to_x(self, g, dy, part):
-        p = self.p
-        zs = pl.ds(4 * part, 4)
-        self.move(g, XS + 2 * dy + part, (self.east, self.west)[part], p.core, zs, self.line(p.xlo, dy))
-
-    def after_y(self, g):
-        p = self.p
-        whole = pl.ds(0, 8)
-        below, above = self.line(p.xlo, 3), self.line(p.xlo, 1)
-        self.landed(g, YS + 0, p.core, whole, below)
-        self.move(g, YS + 2, self.up, p.core, pl.ds(0, 4), below)
-        self.landed(g, YS + 1, p.core, whole, above)
-        self.move(g, YS + 3, self.down, p.core, pl.ds(4, 4), above)
+            self.landed(ZS + d - 1, (p.z + 8 - d) % 8, self.line(0, 0))
+
+    def after_z(self):
+        self.z_landed()
+        own = self.line(0, 0)
+        self.move(YS + 0, self.up, self.whole, own)
+        self.move(YS + 1, self.down, self.whole, own)
+        self.to_x(0, 0)
+        self.to_x(0, 1)
+        self.move(SS + 0, self.twin, self.whole, own)
+
+    def to_x(self, dy, part):
+        self.move(XS + 2 * dy + part, (self.east, self.west)[part], self.parts[part], self.line(0, dy))
+
+    def after_y(self):
+        below, above = self.line(0, 3), self.line(0, 1)
+        self.landed(YS + 0, self.whole, below)
+        self.move(YS + 2, self.up, self.parts[0], below)
+        self.landed(YS + 1, self.whole, above)
+        self.move(YS + 3, self.down, self.parts[1], above)
         for dy in (3, 1):
             for part in (0, 1):
-                self.to_x(g, dy, part)
-        self.move(g, SS + 1, self.twin, p.core, whole, below)
-        self.move(g, SS + 2, self.twin, p.core, whole, above)
-
-    def after_far(self, g):
-        p = self.p
-        far = self.line(p.xlo, 2)
+                self.to_x(dy, part)
+        self.move(SS + 1, self.twin, self.whole, below)
+        self.move(SS + 2, self.twin, self.whole, above)
+
+    def after_far(self):
         for part in (0, 1):
-            zs = pl.ds(4 * part, 4)
-            self.landed(g, YS + 2 + part, p.core, zs, far)
-            self.to_x(g, 2, part)
-            self.move(g, SS + 3 + part, self.twin, p.core, zs, far)
-
-    def after_x(self, g):
-        p = self.p
+            self.landed(YS + 2 + part, self.parts[part], self.line(0, 2))
+            self.to_x(2, part)
+            self.move(SS + 3 + part, self.twin, self.parts[part], self.line(0, 2))
+
+    def after_x(self):
         for dy in (0, 3, 1, 2):
             for part in (0, 1):
-                zs = pl.ds(4 * part, 4)
-                line = self.line(1 - p.xlo, dy)
-                self.landed(g, XS + 2 * dy + part, p.core, zs, line)
-                self.move(g, SS + 5 + 2 * dy + part, self.twin, p.core, zs, line)
-
-    def finish(self, g):
+                self.landed(XS + 2 * dy + part, self.parts[part], self.line(1, dy))
+                self.move(SS + 5 + 2 * dy + part, self.twin, self.parts[part], self.line(1, dy))
+
+    def finish(self):
+        half = 1 - self.p.core
+        self.landed(SS + 0, self.whole, self.line(0, 0), half)
+        self.landed(SS + 1, self.whole, self.line(0, 3), half)
+        self.landed(SS + 2, self.whole, self.line(0, 1), half)
+        for part in (0, 1):
+            self.landed(SS + 3 + part, self.parts[part], self.line(0, 2), half)
+            for dy in range(4):
+                self.landed(SS + 5 + 2 * dy + part, self.parts[part], self.line(1, dy), half)
+
+
+class GatherZXY(Gather):
+    def after_z(self):
+        self.z_landed()
+        own = self.line(0, 0)
+        self.to_x(0, 0)
+        self.to_x(0, 1)
+        self.move(YS + 0, self.up, self.whole, own)
+        self.move(YS + 1, self.down, self.whole, own)
+        self.move(SS + 0, self.twin, self.whole, own)
+
+    def after_x(self):
+        other = self.line(1, 0)
+        for part in (0, 1):
+            self.landed(XS + part, self.parts[part], other)
+        self.move(YS + 4, self.up, self.whole, other)
+        self.move(YS + 5, self.down, self.whole, other)
+        self.move(SS + 5, self.twin, self.whole, other)
+
+    def after_y(self):
+        for k in (0, 1):
+            below, above = self.line(k, 3), self.line(k, 1)
+            self.landed(YS + 4 * k, self.whole, below)
+            self.move(YS + 4 * k + 2, self.up, self.parts[0], below)
+            self.landed(YS + 4 * k + 1, self.whole, above)
+            self.move(YS + 4 * k + 3, self.down, self.parts[1], above)
+            self.move(SS + 5 * k + 1, self.twin, self.whole, below)
+            self.move(SS + 5 * k + 2, self.twin, self.whole, above)
+
+    def after_far(self):
+        for k in (0, 1):
+            for part in (0, 1):
+                self.landed(YS + 4 * k + 2 + part, self.parts[part], self.line(k, 2))
+                self.move(SS + 5 * k + 3 + part, self.twin, self.parts[part], self.line(k, 2))
+
+    def finish(self):
+        half = 1 - self.p.core
+        for k in (0, 1):
+            self.landed(SS + 5 * k, self.whole, self.line(k, 0), half)
+            self.landed(SS + 5 * k + 1, self.whole, self.line(k, 3), half)
+            self.landed(SS + 5 * k + 2, self.whole, self.line(k, 1), half)
+            for part in (0, 1):
+                self.landed(SS + 5 * k + 3 + part, self.parts[part], self.line(k, 2), half)
+
+
+class GatherXYZ(Gather):
+    def quarter(self, part):
+        depth = self.full.shape[-1] // 2
+        return pl.ds(0, self.full.shape[-2]), pl.ds(part * depth, depth)
+
+    def start(self):
         p = self.p
-        half = 1 - p.core
-        whole = pl.ds(0, 8)
-        self.landed(g, SS + 0, half, whole, self.line(p.xlo, 0))
-        self.landed(g, SS + 1, half, whole, self.line(p.xlo, 3))
-        self.landed(g, SS + 2, half, whole, self.line(p.xlo, 1))
         for part in (0, 1):
-            zs = pl.ds(4 * part, 4)
-            self.landed(g, SS + 3 + part, half, zs, self.line(p.xlo, 2))
-            for dy in range(4):
-                self.landed(g, SS + 5 + 2 * dy + part, half, zs, self.line(1 - p.xlo, dy))
-
-    def drain(self, g):
+            mine = self.full.at[p.core, p.z, self.line(0, 0)].at[self.quarter(part)]
+            c = self.copy(XS + part, mine, (self.east, self.west)[part])
+            c.start()
+            self.sent.append(c)
+
+    def after_x(self):
         p = self.p
-
-        def sent(slot, src):
-            self.copy(g, slot, src, src, self.twin).wait_send()
-
+        for part in (0, 1):
+            other = self.full.at[p.core, p.z, self.line(1, 0)].at[self.quarter(part)]
+            self.copy(XS + part, other, self.twin).wait_recv()
+        for k in (0, 1):
+            for d in range(1, 4):
+                self.move(YS + 3 * k + d - 1, p.at(y=(p.y + d) % 4), p.z, self.line(k, 0))
+
+    def after_y(self):
+        p = self.p
+        for k in (0, 1):
+            for d in range(1, 4):
+                self.landed(YS + 3 * k + d - 1, p.z, self.line(k, 4 - d))
         for d in range(1, 8):
-            sent(ZS + d - 1, self.shard[g].at[p.core])
-        whole = self.full[g].at[p.core, pl.ds(0, 8), 0]
-        half = self.full[g].at[p.core, pl.ds(0, 4), 0]
-        for slot in (YS, YS + 1, SS, SS + 1, SS + 2):
-            sent(slot, whole)
-        for slot in (YS + 2, YS + 3, SS + 3, SS + 4):
-            sent(slot, half)
-        for k in range(8):
-            sent(XS + k, half)
-            sent(SS + 5 + k, half)
+            self.move(ZS + d - 1, p.at(z=(p.z + d) % 8), p.z, self.whole)
+        self.move(SS + 0, self.twin, p.z, self.whole)
+
+    def after_z(self):
+        p = self.p
+        for d in range(1, 8):
+            self.landed(ZS + d - 1, (p.z + 8 - d) % 8, self.whole)
+            self.move(SS + d, self.twin, (p.z + 8 - d) % 8, self.whole)
+
+    def finish(self):
+        p = self.p
+        for d in range(8):
+            self.landed(SS + d, (p.z + 8 - d) % 8, self.whole, 1 - p.core)
 
 
 def times(a, b):
@@ -210,8 +277,10 @@
 
 
 def block_kernel(
-    shard0, shard1, shard2, shard3, emb, gain1, gain_merge, gain2, bias1_hbm, bias2_hbm,
+    tok, land, surface, table, levels, gain1, wqkv1, wout1, gain_merge, wmerge, gain2, wqkv2, wout2,
+    bias1_hbm, bias2_hbm,
     one, two,
+    emb,
     full0, full1, full2, full3, flat1, flat2, table1, table2, mask,
     e1, first1, south1, rw1, rn1, rc1, bw1, bn1, bc1, qw, ow, x1, qkv1, s1, mg, mn,
     s2, e2, first2, south2, rw2, rn2, rc2, bw2, bn2, bc2, x2, qkv2,
@@ -220,11 +289,12 @@
 ):
     p = Place()
     full = (full0, full1, full2, full3)
-    net = Gather(p, (shard0, shard1, shard2, shard3), full, send, recv)
+    kinds = (Gather, Gather, Gather, Gather)
+    n0, n1, n2, n3 = nets = [kinds[g](p, g, full[g], send, recv) for g in range(NG)]
     north, south = (p.lat + 63) % 64, (p.lat + 1) % 64
     west, east = (p.lon + 3) % 4, (p.lon + 1) % 4
     around = [(p.lat, west), (north, p.lon), (north, west), (p.lat, east), (south, p.lon), (south, east)]
-    partners = net.partners + around
+    partners = n0.partners + around
     barrier = pltpu.get_barrier_semaphore()
     for to in partners:
         pl.semaphore_signal(barrier, inc=1, device_id=to, device_id_type=MESH)
@@ -232,6 +302,18 @@
     b2 = pltpu.make_async_copy(bias2_hbm, flat2, local.at[1])
     b1.start()
     b2.start()
+
+    own = n0.line(0, 0)
+
+    def halved(w):
+        depth = w.shape[1] // 2
+        return w[:, pl.ds(pl.multiple_of(p.core * depth, depth), depth)]
+
+    full0[p.core, p.z, own] = jnp.concatenate(
+        [halved(wqkv1).astype(jnp.float32), halved(wout1).astype(jnp.float32)], 0).astype(jnp.bfloat16)
+    full1[p.core, p.z, own] = halved(wmerge)
+    full2[p.core, p.z, own] = halved(wqkv2)
+    full3[p.core, p.z, own] = halved(wout2)
     pl.semaphore_wait(barrier, len(partners))
 
     def neighbour(slot, src, dst, way):
@@ -239,19 +321,23 @@
             src_ref=src, dst_ref=dst, send_sem=hsend.at[slot], recv_sem=hrecv.at[slot],
             device_id=around[way], device_id_type=MESH)
 
-    owns = []
-    for g in range(NG):
-        own = pltpu.make_async_copy(
-            net.shard[g].at[p.core], full[g].at[p.core, p.z, net.line(p.xlo, 0)], local.at[2 + g])
-        own.start()
-        owns.append(own)
-    net.start(0)
-
+
+    n0.start()
+    n1.start()
     sixteen = lax.broadcasted_iota(jnp.int32, (16, 512), 0)
     sixteen2 = lax.broadcasted_iota(jnp.int32, (16, 1024), 0)
 
+    numbers = lax.broadcasted_iota(jnp.int32, levels.shape, 0)
+    rows = [jnp.sum(jnp.where(numbers == table[i], levels[...], 0.0), 0, keepdims=True) for i in range(2)]
+    level = jnp.where(lax.broadcasted_iota(jnp.int32, (48, 512), 0) % 2 == 0, rows[0], rows[1])
+    patch = lax.broadcasted_iota(jnp.int32, (48, 24), 0) // 2 == lax.broadcasted_iota(jnp.int32, (48, 24), 1)
+
     def row_norm(r):
-        v = emb[pl.ds(pl.multiple_of(r * 48, 16), 48), :]
+        kinds = land[pl.ds(r, 1), :].astype(jnp.float32)
+        kind = jnp.sum(jnp.where(patch, kinds, 0.0), -1, keepdims=True)
+        ground = jnp.where(kind == 0.0, surface[0:1, :], jnp.where(kind == 1.0, surface[1:2, :], surface[2:3, :]))
+        v = tok[pl.ds(r * 24, 24)].astype(jnp.float32).reshape(48, 512) + ground + level
+        emb[pl.ds(pl.multiple_of(r * 48, 16), 48), :] = v
         n = norm_groups([v[:, 128 * k:128 * k + 128] for k in range(4)], gain1[...])
         e1[r, 0:8, :] = jnp.zeros((8, 512), jnp.float32)
         e1[r, 48:64, :] = jnp.zeros((16, 512), jnp.float32)
@@ -266,29 +352,23 @@
              neighbour(2, first1.at[pl.ds(0, 3)], rc1, 2)]
     for c in halo1:
         c.start()
-    for own in owns:
-        own.wait()
-    net.after_z(0)
-    net.start(1)
-
+
+    n0.after_z()
+    n2.start()
     half = lambda axis: lax.broadcasted_iota(jnp.int32, (WT, 256), axis) >= WT // 2
     cut = (half(0) != half(1)) & (p.lat == 63)
     mask[0] = jnp.zeros((WT, 256), jnp.float32)
     mask[1] = jnp.where(cut, ABSENT, 0.0)
     b1.wait()
     prepare_bias(flat1, table1, 16)
-    net.after_y(0)
-    net.after_z(1)
-    net.start(2)
-    net.after_far(0)
-    net.after_y(1)
+    n0.after_y()
+    n1.after_z()
     b2.wait()
     prepare_bias(flat2, table2, 32)
-    net.after_x(0)
-    net.after_z(2)
-    net.start(3)
-    net.after_far(1)
-
+
+    n0.after_far()
+    n2.after_z()
+    n0.after_x()
     for c in halo1:
         c.wait_recv()
 
@@ -305,8 +385,9 @@
         x1[WT * w:WT * w + WT, :] = e1[3 + 6 * a:9 + 6 * a, 16 + 24 * b:40 + 24 * b, :].reshape(
             WT, 512).astype(jnp.bfloat16)
 
-    net.finish(0)
-
+
+    n1.after_y()
+    n0.finish()
     def unpack(i):
         z, l = i // 4, 2 * (i % 4)
         both = [jnp.concatenate([full0[0, z, l + d], full0[1, z, l + d]], 1).astype(jnp.float32)
@@ -324,9 +405,6 @@
         qkv1[2 * n + 1] = out[:, 128:]
 
     loop(6, project1)
-    net.after_x(1)
-    net.after_y(2)
-    net.after_z(3)
 
     def attend1(i):
         w, g = 3 - i // 4, i % 4
@@ -344,8 +422,6 @@
     back1 = [neighbour(3, bn1, sn1, 4), neighbour(4, bc1, sc1, 5)]
     for c in back1:
         c.start()
-    net.after_far(2)
-    net.after_y(3)
     loop(12, attend1, 8)
 
     def last_columns(r):
@@ -354,10 +430,12 @@
     loop(9, last_columns)
     back1.append(neighbour(5, bw1, sw1, 3))
     back1[2].start()
-    net.after_x(2)
+    n3.start()
+    n1.after_far()
+    n2.after_y()
     loop(16, attend1, 12)
-    net.after_far(3)
-    net.finish(1)
+    n1.after_x()
+    n3.after_z()
     for c in back1:
         c.wait_recv()
 
@@ -376,7 +454,7 @@
     for n in range(2):
         cols = slice(256 * n, 256 * n + 256)
         out = emb[:, cols] + times(x1[...], ow[cols, :])
-        one[:, cols] = out.astype(jnp.bfloat16)
+        one[:, :, cols] = out.reshape(288, 2, 256).astype(jnp.bfloat16)
         s1[2 * n] = out[:, :128]
         s1[2 * n + 1] = out[:, 128:]
 
@@ -398,6 +476,7 @@
 
     loop(9, merge_norm)
 
+    n1.finish()
     def merge_product(n):
         zs = pl.ds(2 * n, 2)
         out = times(mn[:, :1024], full1[0, zs].reshape(256, 1024))
@@ -406,8 +485,8 @@
         s2[2 * n + 1] = out[:, 128:]
 
     loop(4, merge_product)
-    net.after_x(3)
-
+
+    n2.after_far()
     def row_norm2(r):
         rows = pl.ds(pl.multiple_of(24 * r, 8), 24)
         n = norm_groups([s2[k, rows, :] for k in range(8)], gain2[...])
@@ -423,7 +502,7 @@
              neighbour(8, first2.at[pl.ds(0, 3)], rc2, 2)]
     for c in halo2:
         c.start()
-    net.finish(2)
+    n2.after_x()
     for c in halo2:
         c.wait_recv()
     for r in range(3):
@@ -432,9 +511,12 @@
         e2[6 + r, 24:40, :] = jnp.where(sixteen2 >= 4, rc2[r].astype(jnp.float32), e2[6 + r, 24:40, :])
     x2[...] = e2[3:9, 16:40, :].reshape(WT, 1024).astype(jnp.bfloat16)
 
+
+    n2.finish()
+    n3.after_y()
     def project2(z):
-        out = times(x2[:, :512], full2[0, z].reshape(384, 512))
-        out = (out + times(x2[:, 512:], full2[1, z].reshape(384, 512))).astype(jnp.bfloat16)
+        first, second = [full2[h, z].reshape(384, 512) for h in range(2)]
+        out = (times(x2[:, :512], first) + times(x2[:, 512:], second)).astype(jnp.bfloat16)
         for k in range(3):
             qkv2[3 * z + k] = out[:, 128 * k:128 * k + 128]
 
@@ -445,21 +527,31 @@
         out = attend(qkv2[g], qkv2[8 + g], qkv2[16 + g], table2[0, heads, :], table2[1, heads, :], mask[1])
         e2[3:9, 16:40, pl.ds(pl.multiple_of(128 * g, 128), 128)] = out.reshape(6, 24, 128)
 
-    loop(8, attend2)
-    for r in range(3):
-        bw2[r] = e2[3 + r, 24:40, :].astype(jnp.bfloat16)
-        bn2[r] = e2[6 + r, 16:32, :].astype(jnp.bfloat16)
-        bc2[r] = e2[6 + r, 24:40, :].astype(jnp.bfloat16)
-    back2 = [neighbour(9, bw2, sw2, 3), neighbour(10, bn2, sn2, 4), neighbour(11, bc2, sc2, 5)]
-    for c in back2:
-        c.start()
-    net.finish(3)
+    n3.after_far()
+    back2 = []
+    for h in range(2):
+        loop(4 * h + 4, attend2, 4 * h)
+        cols = slice(512 * h, 512 * h + 512)
+        for r in range(3):
+            bw2[h, r] = e2[3 + r, 24:40, cols].astype(jnp.bfloat16)
+            bn2[h, r] = e2[6 + r, 16:32, cols].astype(jnp.bfloat16)
+            bc2[h, r] = e2[6 + r, 24:40, cols].astype(jnp.bfloat16)
+        some = [neighbour(9 + 3 * h, bw2.at[h], sw2.at[h], 3), neighbour(10 + 3 * h, bn2.at[h], sn2.at[h], 4),
+                neighbour(11 + 3 * h, bc2.at[h], sc2.at[h], 5)]
+        for c in some:
+            c.start()
+        if h == 0:
+            n3.after_x()
+        back2 += some
+    n3.finish()
     for c in back2:
         c.wait_recv()
-    for r in range(3):
-        e2[3 + r, 0:16, :] = jnp.where(sixteen2 >= 4, sw2[r].astype(jnp.float32), e2[3 + r, 0:16, :])
-        e2[r, 16:32, :] = sn2[r].astype(jnp.float32)
-        e2[r, 0:16, :] = sc2[r].astype(jnp.float32)
+    for h in range(2):
+        cols = slice(512 * h, 512 * h + 512)
+        for r in range(3):
+            e2[3 + r, 0:16, cols] = jnp.where(sixteen >= 4, sw2[h, r].astype(jnp.float32), e2[3 + r, 0:16, cols])
+            e2[r, 16:32, cols] = sn2[h, r].astype(jnp.float32)
+            e2[r, 0:16, cols] = sc2[h, r].astype(jnp.float32)
     for r in range(6):
         x2[24 * r:24 * r + 24, :] = e2[r, 4:28, :].astype(jnp.bfloat16)
 
@@ -473,25 +565,17 @@
     loop(4, last)
     for c in halo1 + back1 + halo2 + back2:
         c.wait_send()
-    for g in range(NG):
-        net.drain(g)
+    for net in nets:
+        net.drain()
 
 
 def shards(
     tokens, land_sea, surface_embed, level_table, level_embed, gain1, w_qkv1, bias1, w_out1,
     gain_merge, w_merge, gain2, w_qkv2, bias2, w_out2,
 ):
-    weights = [jnp.concatenate([w_qkv1, w_out1], 1), w_merge, w_qkv2, w_out2]
-    weights = [w.T.reshape(w.shape[1], 2, w.shape[0] // 2).transpose(1, 0, 2) for w in weights]
-    kind = land_sea[:, :, None, None]
-    surface = jnp.where(kind == 0, surface_embed[0], jnp.where(kind == 1, surface_embed[1], surface_embed[2]))
-    numbers = jnp.arange(level_embed.shape[0], dtype=jnp.int32)
-    level_rows = jnp.sum(
-        jnp.where((level_table[:, None] == numbers)[:, :, None], level_embed[None], 0.0), 1)
-    embedded = tokens.astype(jnp.float32) + surface + level_rows[None, None]
     f32, bf16 = jnp.float32, jnp.bfloat16
     shapes = [(2, 8, 8, rows, depth // 2) for rows, depth in GROUPS]
-    scratch = [pltpu.VMEM(s, bf16) for s in shapes] + [pltpu.VMEM(s, t) for s, t in (
+    scratch = [pltpu.VMEM((576, 512), f32)] + [pltpu.VMEM(s, bf16) for s in shapes] + [pltpu.VMEM(s, t) for s, t in (
         ((16, WT * WT), f32), ((32, WT * WT), f32),
         ((2, 16 * WT, 128), f32), ((2, 32 * WT, 128), f32), ((2, WT, 256), f32),
         ((15, 64, 512), f32), ((12, 16, 512), bf16), ((3, 48, 512), bf16),
@@ -501,24 +585,25 @@
         ((4, 576, 128), f32), ((16, WT, 128), f32), ((WT, 2048), bf16),
         ((8, WT, 128), f32), ((9, 40, 1024), f32), ((6, 16, 1024), bf16), ((6, 16, 1024), bf16),
         ((3, 16, 1024), bf16), ((3, 16, 1024), bf16), ((3, 16, 1024), bf16),
-        ((3, 16, 1024), bf16), ((3, 16, 1024), bf16), ((3, 16, 1024), bf16),
+        ((2, 3, 16, 512), bf16), ((2, 3, 16, 512), bf16), ((2, 3, 16, 512), bf16),
         ((WT, 1024), bf16), ((24, WT, 128), bf16),
         ((9, 16, 512), bf16), ((3, 48, 512), bf16), ((3, 16, 512), bf16),
-        ((3, 16, 1024), bf16), ((3, 16, 1024), bf16), ((3, 16, 1024), bf16),
+        ((2, 3, 16, 512), bf16), ((2, 3, 16, 512), bf16), ((2, 3, 16, 512), bf16),
     )] + [
         pltpu.SemaphoreType.DMA((NG, SLOTS)), pltpu.SemaphoreType.DMA((NG, SLOTS)),
-        pltpu.SemaphoreType.DMA((12,)), pltpu.SemaphoreType.DMA((12,)), pltpu.SemaphoreType.DMA((6,)),
+        pltpu.SemaphoreType.DMA((15,)), pltpu.SemaphoreType.DMA((15,)), pltpu.SemaphoreType.DMA((2,)),
     ]
     vmem, anywhere = pl.BlockSpec(memory_space=pltpu.VMEM), pl.BlockSpec(memory_space=pl.ANY)
     one, two = pl.pallas_call(
         block_kernel,
-        out_shape=[jax.ShapeDtypeStruct((576, 512), bf16), jax.ShapeDtypeStruct((WT, 1024), bf16)],
-        in_specs=[vmem] * 8 + [anywhere] * 2,
+        out_shape=[jax.ShapeDtypeStruct((288, 2, 512), bf16), jax.ShapeDtypeStruct((WT, 1024), bf16)],
+        in_specs=[vmem] * 3 + [pl.BlockSpec(memory_space=pltpu.SMEM)] + [vmem] * 9 + [anywhere] * 2,
         out_specs=[vmem] * 2,
         scratch_shapes=scratch,
         compiler_params=pltpu.CompilerParams(
             collective_id=0, has_side_effects=True, vmem_limit_bytes=60 * 2**20),
-    )(*weights, embedded.reshape(576, 512), gain1[None], gain_merge[None], gain2[None], bias1, bias2)
+    )(tokens.reshape(288, 2, 512), land_sea, surface_embed, level_table, level_embed, gain1[None], w_qkv1.T,
+      w_out1.T, gain_merge[None], w_merge.T, gain2[None], w_qkv2.T, w_out2.T, bias1, bias2)
     return one.reshape(12, 24, 2, 512), two.reshape(6, 12, 2, 1024)
 
 

time: 117 us -> 97.1 us (0.83)
  Pallas kernels: 103 us -> 92.1 us
  local copies, waits for them, and re-layouts: 8.63 us -> 4.16 us
  other arithmetic: 4.1 us -> 0 us
    pallas_call x1, Pallas kernels: 103 us -> 92.1 us  [shards(): pl.pallas_call(block_kernel, out_shape=[jax.ShapeDtypeStruct((288, 2, 512...]
    reshape x5 -> x0, local copies, waits for them, and re-layouts: 4.34 us -> none  [the longest x4 2.51 us: shards(): w.T.reshape(w.shape[1], 2, w.shape[0] // 2).transpose(1, 0, 2)]
    unnamed x12 -> x1, local copies, waits for them, and re-layouts: 0.04 us -> 2.37 us
    add x1 -> x0, other arithmetic: 1.73 us -> none  [shards(): embedded = tokens.astype(jnp.float32) + surface + level_rows[None, None]]
    reshape x2 -> x1, local copies, waits for them, and re-layouts: 3.43 us -> 1.79 us  [shards(): return (one.reshape(12, 24, 2, 512), two.reshape(6, 12, 2, 1024))]
    eq x2 -> x0, other arithmetic: 1.37 us -> none  [the longest x1 0.7 us: shards(): kind == 0]
where the time goes in v3:
time: 97.1 us; the launch traced here: 96.9 us
  Pallas kernels  92.1 us (95%)
  local copies, waits for them, and re-layouts  4.16 us (4%)
    pallas_call x1, Pallas kernels, shards(): pl.pallas_call(block_kernel, out_shape=[jax.ShapeDtypeStruct((288, 2, 512...  92.1 us
    unnamed x1, local copies, waits for them, and re-layouts  2.37 us

profile of v3, /device:TPU:1, one launch (start us, length us, event | category | flops | bytes accessed | tf_op | source)
XLA Modules:
  0.0 96.9 jit_solution(16763770607517579749)
XLA Ops:
  0.6 92.1 %shard_map.158 = (bf16[288,2,512]{2,1,0:T(2,128)(2,1)}, bf16[144,1024]{1,0:T(8,128)(2,1)}) custom-call(bf16[288,2,512]{2,1,0:T(2,128)(2,1)} %bitcast.11, s32[12,24]{1,0:T(8,128)} %land.1, f32[3,512]{1,0:T(4,128)} %surface.1, s32[2]{0:T(128)} %table.1, f32[13,512]{1,0:T(8,128)} %levels.1, f32[1,512]{1,0:T(1,128)} %bitcast.19, bf16[24,512]{1,0:T(8,128)(2,1)} %bitcast.15, ...), custom_call_target="tpu_custom_call" | custom-call | tf_op jit(solution)/shard_map/pallas_call | solution.py:597
  92.7 1.8 %reshape.15 = bf16[6,12,2,1024]{3,2,1,0:T(2,128)(2,1)} reshape(bf16[144,1024]{1,0:T(8,128)(2,1)} %get-tuple-element.5) | data formatting | bytes 589824 | tf_op jit(solution)/shard_map/reshape | solution.py:607
  94.5 2.4 %copy.18 = bf16[12,24,2,512]{3,2,1,0:T(2,128)(2,1)} copy(bf16[12,24,2,512]{3,2,1,0:T(2,128)(2,1)} %bitcast.10) | data formatting | bytes 1179648

commit v4 on v3

--- a/solution.py
+++ b/solution.py
@@ -272,18 +272,19 @@
     return total / over
 
 
-def loop(count, step, first=0):
-    lax.fori_loop(first, count, lambda i, c: (step(i), c)[1], 0)
+def loop(count, step, first=0, unroll=1):
+    lax.fori_loop(first, count, lambda i, c: (step(i), c)[1], 0, unroll=unroll)
 
 
 def block_kernel(
-    tok, land, surface, table, levels, gain1, wqkv1, wout1, gain_merge, wmerge, gain2, wqkv2, wout2,
-    bias1_hbm, bias2_hbm,
+    tok_hbm, land_hbm, surface_hbm, table, levels_hbm, gain1_hbm, wqkv1_hbm, wout1_hbm, gain_merge_hbm,
+    wmerge_hbm, gain2_hbm, wqkv2_hbm, wout2_hbm, bias1_hbm, bias2_hbm,
     one, two,
+    tok, land, surface, levels, gain1, wqkv1, wout1, gain_merge, wmerge, gain2, wqkv2, wout2,
     emb,
     full0, full1, full2, full3, flat1, flat2, table1, table2, mask,
-    e1, first1, south1, rw1, rn1, rc1, bw1, bn1, bc1, qw, ow, x1, qkv1, s1, mg, mn,
-    s2, e2, first2, south2, rw2, rn2, rc2, bw2, bn2, bc2, x2, qkv2,
+    pad, e1, hw1, hn1, hc1, rw1, rn1, rc1, bw1, bn1, bc1, qw, ow, x1, qkv1, s1, mg, mn,
+    s2, e2, hw2, hn2, hc2, rw2, rn2, rc2, bw2, bn2, bc2, x2, qkv2,
     sw1, sn1, sc1, sw2, sn2, sc2,
     send, recv, hsend, hrecv, local,
 ):
@@ -298,10 +299,20 @@
     barrier = pltpu.get_barrier_semaphore()
     for to in partners:
         pl.semaphore_signal(barrier, inc=1, device_id=to, device_id_type=MESH)
+    pairs = (
+        (wqkv1_hbm, wqkv1), (wout1_hbm, wout1), (tok_hbm, tok), (land_hbm, land), (surface_hbm, surface),
+        (levels_hbm, levels), (gain1_hbm, gain1), (wmerge_hbm, wmerge), (wqkv2_hbm, wqkv2), (wout2_hbm, wout2),
+        (gain_merge_hbm, gain_merge), (gain2_hbm, gain2))
+    inputs = [pltpu.make_async_copy(src, dst, local.at[2 + i]) for i, (src, dst) in enumerate(pairs)]
+    for c in inputs:
+        c.start()
     b1 = pltpu.make_async_copy(bias1_hbm, flat1, local.at[0])
     b2 = pltpu.make_async_copy(bias2_hbm, flat2, local.at[1])
     b1.start()
     b2.start()
+
+    for c in inputs:
+        c.wait()
 
     own = n0.line(0, 0)
 
@@ -324,8 +335,20 @@
 
     n0.start()
     n1.start()
-    sixteen = lax.broadcasted_iota(jnp.int32, (16, 512), 0)
-    sixteen2 = lax.broadcasted_iota(jnp.int32, (16, 1024), 0)
+    n2.start()
+
+    def pack(out, source, count, rows, first):
+        for i, r in enumerate(rows):
+            pad[count * i:count * i + count, :] = source[r, first:first + count, :]
+        out[...] = pad[:out.shape[0], :].astype(jnp.bfloat16)
+
+    def unpack_rows(target, came, count, rows, first):
+        pad[:came.shape[0], :] = came[...].astype(jnp.float32)
+        for i, r in enumerate(rows):
+            target[r, first:first + count, :] = pad[count * i:count * i + count, :]
+
+    pad[...] = jnp.zeros((112, 512), jnp.float32)
+    own_rows, first_rows, next_rows = range(3, 12), range(3), range(12, 15)
 
     numbers = lax.broadcasted_iota(jnp.int32, levels.shape, 0)
     rows = [jnp.sum(jnp.where(numbers == table[i], levels[...], 0.0), 0, keepdims=True) for i in range(2)]
@@ -339,22 +362,18 @@
         v = tok[pl.ds(r * 24, 24)].astype(jnp.float32).reshape(48, 512) + ground + level
         emb[pl.ds(pl.multiple_of(r * 48, 16), 48), :] = v
         n = norm_groups([v[:, 128 * k:128 * k + 128] for k in range(4)], gain1[...])
-        e1[r, 0:8, :] = jnp.zeros((8, 512), jnp.float32)
-        e1[r, 48:64, :] = jnp.zeros((16, 512), jnp.float32)
         for k in range(4):
             e1[r, 4:52, 128 * k:128 * k + 128] = n[k]
-        first1[r] = e1[r, 0:16, :].astype(jnp.bfloat16)
 
     loop(12, row_norm)
-    for r in range(3):
-        south1[r] = e1[r, 16:64, :].astype(jnp.bfloat16)
-    halo1 = [neighbour(0, first1.at[pl.ds(3, 9)], rw1, 0), neighbour(1, south1, rn1, 1),
-             neighbour(2, first1.at[pl.ds(0, 3)], rc1, 2)]
+    pack(hw1, e1, 12, own_rows, 4)
+    pack(hn1, e1, 36, first_rows, 16)
+    pack(hc1, e1, 12, first_rows, 4)
+    halo1 = [neighbour(0, hw1, rw1, 0), neighbour(1, hn1, rn1, 1), neighbour(2, hc1, rc1, 2)]
     for c in halo1:
         c.start()
 
     n0.after_z()
-    n2.start()
     half = lambda axis: lax.broadcasted_iota(jnp.int32, (WT, 256), axis) >= WT // 2
     cut = (half(0) != half(1)) & (p.lat == 63)
     mask[0] = jnp.zeros((WT, 256), jnp.float32)
@@ -372,14 +391,9 @@
     for c in halo1:
         c.wait_recv()
 
-    def take_west(r):
-        e1[r + 3, 48:64, :] = jnp.where(sixteen >= 4, rw1[r].astype(jnp.float32), e1[r + 3, 48:64, :])
-
-    loop(9, take_west)
-    for r in range(3):
-        n = rn1[r].astype(jnp.float32)
-        e1[12 + r, 16:48, :] = n[:32]
-        e1[12 + r, 48:64, :] = jnp.where(sixteen >= 4, rc1[r].astype(jnp.float32), n[32:])
+    unpack_rows(e1, rw1, 12, own_rows, 52)
+    unpack_rows(e1, rn1, 36, next_rows, 16)
+    unpack_rows(e1, rc1, 12, next_rows, 52)
     for w in range(4):
         a, b = w // 2, w % 2
         x1[WT * w:WT * w + WT, :] = e1[3 + 6 * a:9 + 6 * a, 16 + 24 * b:40 + 24 * b, :].reshape(
@@ -415,37 +429,29 @@
         e1[pl.ds(3 + 6 * (w // 2), 6), pl.ds(pl.multiple_of(16 + 24 * (w % 2), 8), 24),
            pl.ds(pl.multiple_of(128 * g, 128), 128)] = out.reshape(6, 24, 128)
 
-    loop(8, attend1)
-    for r in range(3):
-        bn1[r] = e1[12 + r, 16:64, :].astype(jnp.bfloat16)
-        bc1[r] = e1[12 + r, 48:64, :].astype(jnp.bfloat16)
+    loop(8, attend1, 0, 2)
+    pack(bn1, e1, 36, next_rows, 16)
+    pack(bc1, e1, 12, next_rows, 52)
     back1 = [neighbour(3, bn1, sn1, 4), neighbour(4, bc1, sc1, 5)]
     for c in back1:
         c.start()
-    loop(12, attend1, 8)
-
-    def last_columns(r):
-        bw1[r] = e1[r + 3, 48:64, :].astype(jnp.bfloat16)
-
-    loop(9, last_columns)
+    loop(12, attend1, 8, 2)
+
+    pack(bw1, e1, 12, own_rows, 52)
     back1.append(neighbour(5, bw1, sw1, 3))
     back1[2].start()
     n3.start()
     n1.after_far()
     n2.after_y()
-    loop(16, attend1, 12)
+    loop(16, attend1, 12, 2)
     n1.after_x()
     n3.after_z()
     for c in back1:
         c.wait_recv()
 
-    def keep_west(r):
-        e1[r + 3, 0:16, :] = jnp.where(sixteen >= 4, sw1[r].astype(jnp.float32), e1[r + 3, 0:16, :])
-
-    loop(9, keep_west)
-    for r in range(3):
-        e1[r, 16:64, :] = sn1[r].astype(jnp.float32)
-        e1[r, 0:16, :] = sc1[r].astype(jnp.float32)
+    unpack_rows(e1, sw1, 12, own_rows, 4)
+    unpack_rows(e1, sn1, 36, first_rows, 16)
+    unpack_rows(e1, sc1, 12, first_rows, 4)
 
     def collect1(r):
         x1[pl.ds(pl.multiple_of(48 * r, 16), 48), :] = e1[r, 4:52, :].astype(jnp.bfloat16)
@@ -454,7 +460,7 @@
     for n in range(2):
         cols = slice(256 * n, 256 * n + 256)
         out = emb[:, cols] + times(x1[...], ow[cols, :])
-        one[:, :, cols] = out.reshape(288, 2, 256).astype(jnp.bfloat16)
+        one[:, cols] = out.astype(jnp.bfloat16)
         s1[2 * n] = out[:, :128]
         s1[2 * n + 1] = out[:, 128:]
 
@@ -469,12 +475,12 @@
     loop(6, merge_rows)
 
     def merge_norm(c):
-        rows = pl.ds(pl.multiple_of(16 * c, 16), 16)
+        rows = pl.ds(pl.multiple_of(48 * c, 16), 48)
         n = norm_groups([mg[k, rows, :] for k in range(16)], gain_merge[...])
         for k in range(16):
             mn[rows, 128 * k:128 * k + 128] = n[k].astype(jnp.bfloat16)
 
-    loop(9, merge_norm)
+    loop(3, merge_norm)
 
     n1.finish()
     def merge_product(n):
@@ -488,32 +494,44 @@
 
     n2.after_far()
     def row_norm2(r):
-        rows = pl.ds(pl.multiple_of(24 * r, 8), 24)
+        rows = pl.ds(pl.multiple_of(72 * r, 8), 72)
         n = norm_groups([s2[k, rows, :] for k in range(8)], gain2[...])
-        e2[r, 0:8, :] = jnp.zeros((8, 1024), jnp.float32)
-        e2[r, 24:40, :] = jnp.zeros((16, 1024), jnp.float32)
         for k in range(8):
-            e2[r, 4:28, 128 * k:128 * k + 128] = n[k]
-        first2[r] = e2[r, 0:16, :].astype(jnp.bfloat16)
-        south2[r] = e2[r, 16:32, :].astype(jnp.bfloat16)
-
-    loop(6, row_norm2)
-    halo2 = [neighbour(6, first2.at[pl.ds(3, 3)], rw2, 0), neighbour(7, south2.at[pl.ds(0, 3)], rn2, 1),
-             neighbour(8, first2.at[pl.ds(0, 3)], rc2, 2)]
+            e2[pl.ds(3 * r, 3), 4:28, 128 * k:128 * k + 128] = n[k].reshape(3, 24, 128)
+
+    loop(2, row_norm2)
+
+    def pack2(out, r, first, lanes, width):
+        for k in range(2):
+            for i in range(3):
+                at = 36 * k + 12 * i
+                pad[at:at + 12, :width] = e2[r + i, first:first + 12, lanes + width * k:lanes + width * k + width]
+        out[...] = pad[:80, :width].astype(jnp.bfloat16)
+
+    def unpack2(came, r, first, lanes, width):
+        pad[:80, :width] = came[...].astype(jnp.float32)
+        for k in range(2):
+            for i in range(3):
+                at = 36 * k + 12 * i
+                e2[r + i, first:first + 12, lanes + width * k:lanes + width * k + width] = pad[at:at + 12, :width]
+
+    pack2(hw2, 3, 4, 0, 512)
+    pack2(hn2, 0, 16, 0, 512)
+    pack2(hc2, 0, 4, 0, 512)
+    halo2 = [neighbour(6, hw2, rw2, 0), neighbour(7, hn2, rn2, 1), neighbour(8, hc2, rc2, 2)]
     for c in halo2:
         c.start()
     n2.after_x()
+    n3.after_y()
     for c in halo2:
         c.wait_recv()
-    for r in range(3):
-        e2[3 + r, 24:40, :] = jnp.where(sixteen2 >= 4, rw2[r].astype(jnp.float32), e2[3 + r, 24:40, :])
-        e2[6 + r, 16:32, :] = rn2[r].astype(jnp.float32)
-        e2[6 + r, 24:40, :] = jnp.where(sixteen2 >= 4, rc2[r].astype(jnp.float32), e2[6 + r, 24:40, :])
+    unpack2(rw2, 3, 28, 0, 512)
+    unpack2(rn2, 6, 16, 0, 512)
+    unpack2(rc2, 6, 28, 0, 512)
     x2[...] = e2[3:9, 16:40, :].reshape(WT, 1024).astype(jnp.bfloat16)
 
 
     n2.finish()
-    n3.after_y()
     def project2(z):
         first, second = [full2[h, z].reshape(384, 512) for h in range(2)]
         out = (times(x2[:, :512], first) + times(x2[:, 512:], second)).astype(jnp.bfloat16)
@@ -527,31 +545,27 @@
         out = attend(qkv2[g], qkv2[8 + g], qkv2[16 + g], table2[0, heads, :], table2[1, heads, :], mask[1])
         e2[3:9, 16:40, pl.ds(pl.multiple_of(128 * g, 128), 128)] = out.reshape(6, 24, 128)
 
-    n3.after_far()
     back2 = []
     for h in range(2):
-        loop(4 * h + 4, attend2, 4 * h)
-        cols = slice(512 * h, 512 * h + 512)
-        for r in range(3):
-            bw2[h, r] = e2[3 + r, 24:40, cols].astype(jnp.bfloat16)
-            bn2[h, r] = e2[6 + r, 16:32, cols].astype(jnp.bfloat16)
-            bc2[h, r] = e2[6 + r, 24:40, cols].astype(jnp.bfloat16)
+        loop(4 * h + 4, attend2, 4 * h, 2)
+        pack2(bw2.at[h], 3, 28, 512 * h, 256)
+        pack2(bn2.at[h], 6, 16, 512 * h, 256)
+        pack2(bc2.at[h], 6, 28, 512 * h, 256)
         some = [neighbour(9 + 3 * h, bw2.at[h], sw2.at[h], 3), neighbour(10 + 3 * h, bn2.at[h], sn2.at[h], 4),
                 neighbour(11 + 3 * h, bc2.at[h], sc2.at[h], 5)]
         for c in some:
             c.start()
         if h == 0:
-            n3.after_x()
+            n3.after_far()
         back2 += some
+    n3.after_x()
     n3.finish()
     for c in back2:
         c.wait_recv()
     for h in range(2):
-        cols = slice(512 * h, 512 * h + 512)
-        for r in range(3):
-            e2[3 + r, 0:16, cols] = jnp.where(sixteen >= 4, sw2[h, r].astype(jnp.float32), e2[3 + r, 0:16, cols])
-            e2[r, 16:32, cols] = sn2[h, r].astype(jnp.float32)
-            e2[r, 0:16, cols] = sc2[h, r].astype(jnp.float32)
+        unpack2(sw2.at[h], 3, 4, 512 * h, 256)
+        unpack2(sn2.at[h], 0, 16, 512 * h, 256)
+        unpack2(sc2.at[h], 0, 4, 512 * h, 256)
     for r in range(6):
         x2[24 * r:24 * r + 24, :] = e2[r, 4:28, :].astype(jnp.bfloat16)
 
@@ -575,35 +589,34 @@
 ):
     f32, bf16 = jnp.float32, jnp.bfloat16
     shapes = [(2, 8, 8, rows, depth // 2) for rows, depth in GROUPS]
-    scratch = [pltpu.VMEM((576, 512), f32)] + [pltpu.VMEM(s, bf16) for s in shapes] + [pltpu.VMEM(s, t) for s, t in (
+    level1 = [((112, 512), bf16), ((112, 512), bf16), ((48, 512), bf16)]
+    operands = (
+        tokens.reshape(288, 2, 512), land_sea, surface_embed, level_table, level_embed, gain1[None], w_qkv1.T,
+        w_out1.T, gain_merge[None], w_merge.T, gain2[None], w_qkv2.T, w_out2.T, bias1, bias2)
+    scratch = [pltpu.VMEM(a.shape, a.dtype) for i, a in enumerate(operands[:13]) if i != 3]
+    scratch += [pltpu.VMEM((576, 512), f32)] + [pltpu.VMEM(s, bf16) for s in shapes] + [pltpu.VMEM(s, t) for s, t in (
         ((16, WT * WT), f32), ((32, WT * WT), f32),
         ((2, 16 * WT, 128), f32), ((2, 32 * WT, 128), f32), ((2, WT, 256), f32),
-        ((15, 64, 512), f32), ((12, 16, 512), bf16), ((3, 48, 512), bf16),
-        ((9, 16, 512), bf16), ((3, 48, 512), bf16), ((3, 16, 512), bf16),
-        ((9, 16, 512), bf16), ((3, 48, 512), bf16), ((3, 16, 512), bf16),
+        ((112, 512), f32), ((15, 64, 512), f32), *level1, *level1, *level1,
         ((1536, 512), bf16), ((512, 512), bf16), ((576, 512), bf16), ((12, 576, 128), bf16),
         ((4, 576, 128), f32), ((16, WT, 128), f32), ((WT, 2048), bf16),
-        ((8, WT, 128), f32), ((9, 40, 1024), f32), ((6, 16, 1024), bf16), ((6, 16, 1024), bf16),
-        ((3, 16, 1024), bf16), ((3, 16, 1024), bf16), ((3, 16, 1024), bf16),
-        ((2, 3, 16, 512), bf16), ((2, 3, 16, 512), bf16), ((2, 3, 16, 512), bf16),
+        ((8, WT, 128), f32), ((9, 40, 1024), f32), *[((80, 512), bf16)] * 6, *[((2, 80, 256), bf16)] * 3,
         ((WT, 1024), bf16), ((24, WT, 128), bf16),
-        ((9, 16, 512), bf16), ((3, 48, 512), bf16), ((3, 16, 512), bf16),
-        ((2, 3, 16, 512), bf16), ((2, 3, 16, 512), bf16), ((2, 3, 16, 512), bf16),
+        *level1, *[((2, 80, 256), bf16)] * 3,
     )] + [
         pltpu.SemaphoreType.DMA((NG, SLOTS)), pltpu.SemaphoreType.DMA((NG, SLOTS)),
-        pltpu.SemaphoreType.DMA((15,)), pltpu.SemaphoreType.DMA((15,)), pltpu.SemaphoreType.DMA((2,)),
+        pltpu.SemaphoreType.DMA((15,)), pltpu.SemaphoreType.DMA((15,)), pltpu.SemaphoreType.DMA((14,)),
     ]
     vmem, anywhere = pl.BlockSpec(memory_space=pltpu.VMEM), pl.BlockSpec(memory_space=pl.ANY)
     one, two = pl.pallas_call(
         block_kernel,
-        out_shape=[jax.ShapeDtypeStruct((288, 2, 512), bf16), jax.ShapeDtypeStruct((WT, 1024), bf16)],
-        in_specs=[vmem] * 3 + [pl.BlockSpec(memory_space=pltpu.SMEM)] + [vmem] * 9 + [anywhere] * 2,
+        out_shape=[jax.ShapeDtypeStruct((576, 512), bf16), jax.ShapeDtypeStruct((WT, 1024), bf16)],
+        in_specs=[anywhere] * 3 + [pl.BlockSpec(memory_space=pltpu.SMEM)] + [anywhere] * 11,
         out_specs=[vmem] * 2,
         scratch_shapes=scratch,
         compiler_params=pltpu.CompilerParams(
             collective_id=0, has_side_effects=True, vmem_limit_bytes=60 * 2**20),
-    )(tokens.reshape(288, 2, 512), land_sea, surface_embed, level_table, level_embed, gain1[None], w_qkv1.T,
-      w_out1.T, gain_merge[None], w_merge.T, gain2[None], w_qkv2.T, w_out2.T, bias1, bias2)
+    )(*operands)
     return one.reshape(12, 24, 2, 512), two.reshape(6, 12, 2, 1024)
 
 

time: 97.1 us -> 91.3 us (0.940)
  Pallas kernels: 92.1 us -> 86.1 us
    pallas_call x1, Pallas kernels: 92.1 us -> 86.1 us  [shards(): pl.pallas_call(block_kernel, out_shape=[jax.ShapeDtypeStruct((576, 512),...]
    reshape x1 -> x2, local copies, waits for them, and re-layouts: 1.79 us -> 4.35 us  [shards(): return (one.reshape(12, 24, 2, 512), two.reshape(6, 12, 2, 1024))]
    unnamed x1 -> x0, local copies, waits for them, and re-layouts: 2.37 us -> none
where the time goes in v4:
time: 91.3 us; the launch traced here: 91.1 us
  Pallas kernels  86.1 us (94%)
  local copies, waits for them, and re-layouts  4.35 us (5%)
    pallas_call x1, Pallas kernels, shards(): pl.pallas_call(block_kernel, out_shape=[jax.ShapeDtypeStruct((576, 512),...  86.1 us
    reshape x2, local copies, waits for them, and re-layouts, shards(): return (one.reshape(12, 24, 2, 512), two.reshape(6, 12, 2, 1024))  4.35 us

profile of v4, /device:TPU:1, one launch (start us, length us, event | category | flops | bytes accessed | tf_op | source)
XLA Modules:
  0.0 91.1 jit_solution(737628525995320268)
XLA Ops:
  0.6 86.1 %shard_map.158 = (bf16[576,512]{1,0:T(8,128)(2,1)}, bf16[144,1024]{1,0:T(8,128)(2,1)}) custom-call(bf16[288,2,512]{2,1,0:T(2,128)(2,1)} %bitcast.9, s32[12,24]{1,0:T(8,128)} %land_hbm.1, f32[3,512]{1,0:T(4,128)} %surface_hbm.1, s32[2]{0:T(128)} %table.1, f32[13,512]{1,0:T(8,128)} %levels_hbm.1, f32[1,512]{1,0:T(1,128)} %bitcast.17, ...), custom_call_target="tpu_custom_call" | custom-call | tf_op jit(solution)/shard_map/pallas_call | solution.py:611
  86.8 2.6 %reshape.14 = bf16[12,24,2,512]{3,2,1,0:T(2,128)(2,1)} reshape(bf16[576,512]{1,0:T(8,128)(2,1)} %get-tuple-element.4) | data formatting | bytes 1179648 | tf_op jit(solution)/shard_map/reshape | solution.py:620
  89.4 1.8 %reshape.15 = bf16[6,12,2,1024]{3,2,1,0:T(2,128)(2,1)} reshape(bf16[144,1024]{1,0:T(8,128)(2,1)} %get-tuple-element.5) | data formatting | bytes 589824 | tf_op jit(solution)/shard_map/reshape | solution.py:620

commit v5 on v4

--- a/solution.py
+++ b/solution.py
@@ -560,23 +560,26 @@
         back2 += some
     n3.after_x()
     n3.finish()
-    for c in back2:
-        c.wait_recv()
     for h in range(2):
+        for c in back2[3 * h:3 * h + 3]:
+            c.wait_recv()
         unpack2(sw2.at[h], 3, 4, 512 * h, 256)
         unpack2(sn2.at[h], 0, 16, 512 * h, 256)
         unpack2(sc2.at[h], 0, 4, 512 * h, 256)
-    for r in range(6):
-        x2[24 * r:24 * r + 24, :] = e2[r, 4:28, :].astype(jnp.bfloat16)
-
-    def last(n):
-        zs = pl.ds(2 * n, 2)
-        out = times(x2[:, :512], full3[0, zs].reshape(256, 512))
-        out = out + times(x2[:, 512:], full3[1, zs].reshape(256, 512))
-        out = out + jnp.concatenate([s2[2 * n], s2[2 * n + 1]], 1)
-        two[:, pl.ds(pl.multiple_of(256 * n, 256), 256)] = out.astype(jnp.bfloat16)
-
-    loop(4, last)
+        cols = slice(512 * h, 512 * h + 512)
+        for r in range(6):
+            x2[24 * r:24 * r + 24, cols] = e2[r, 4:28, cols].astype(jnp.bfloat16)
+
+        def last(n):
+            out = times(x2[:, cols], full3[h, pl.ds(2 * n, 2)].reshape(256, 512))
+            out = out + jnp.concatenate([s2[2 * n], s2[2 * n + 1]], 1)
+            if h == 0:
+                s2[2 * n] = out[:, :128]
+                s2[2 * n + 1] = out[:, 128:]
+            else:
+                two[:, pl.ds(pl.multiple_of(256 * n, 256), 256)] = out.astype(jnp.bfloat16)
+
+        loop(4, last)
     for c in halo1 + back1 + halo2 + back2:
         c.wait_send()
     for net in nets:

time: 91.3 us -> 91.1 us (level)
  no operation moved by 1% of the time
where the time goes in v5:
time: 91.1 us; the launch traced here: 91 us
  Pallas kernels  86 us (94%)
  local copies, waits for them, and re-layouts  4.35 us (5%)
    pallas_call x1, Pallas kernels, shards(): pl.pallas_call(block_kernel, out_shape=[jax.ShapeDtypeStruct((576, 512),...  86 us
    reshape x2, local copies, waits for them, and re-layouts, shards(): return (one.reshape(12, 24, 2, 512), two.reshape(6, 12, 2, 1024))  4.35 us

profile of v5, /device:TPU:1, one launch (start us, length us, event | category | flops | bytes accessed | tf_op | source)
XLA Modules:
  0.0 91.0 jit_solution(14869078793879716312)
XLA Ops:
  0.6 86.0 %shard_map.158 = (bf16[576,512]{1,0:T(8,128)(2,1)}, bf16[144,1024]{1,0:T(8,128)(2,1)}) custom-call(bf16[288,2,512]{2,1,0:T(2,128)(2,1)} %bitcast.9, s32[12,24]{1,0:T(8,128)} %land_hbm.1, f32[3,512]{1,0:T(4,128)} %surface_hbm.1, s32[2]{0:T(128)} %table.1, f32[13,512]{1,0:T(8,128)} %levels_hbm.1, f32[1,512]{1,0:T(1,128)} %bitcast.17, ...), custom_call_target="tpu_custom_call" | custom-call | tf_op jit(solution)/shard_map/pallas_call | solution.py:614
  86.6 2.6 %reshape.14 = bf16[12,24,2,512]{3,2,1,0:T(2,128)(2,1)} reshape(bf16[576,512]{1,0:T(8,128)(2,1)} %get-tuple-element.4) | data formatting | bytes 1179648 | tf_op jit(solution)/shard_map/reshape | solution.py:623
  89.2 1.8 %reshape.15 = bf16[6,12,2,1024]{3,2,1,0:T(2,128)(2,1)} reshape(bf16[144,1024]{1,0:T(8,128)(2,1)} %get-tuple-element.5) | data formatting | bytes 589824 | tf_op jit(solution)/shard_map/reshape | solution.py:623
